TPU v7x, 32 devices: a whole 2x2x4 slice. The times are simulated.
32 devices in a mesh: pipe: 2 (over core), ctx: 16 (over z, y, x).
Axes of the slice: x: 2, y: 2, z: 4, core: 2. Of those that a mesh axis runs over, the one named last changes fastest.
Arguments:
- saved: bfloat16 [2, 2048, 4096], P('pipe', 'ctx'), may hold values from -6 to 6
- grad_out: bfloat16 [2048, 4096], P('ctx'), may hold values from -6 to 6
- route_blocks: int32 [2, 16, 2], P('pipe', 'ctx'), may hold values from 0 to 31, as said below
- route_dest: int32 [2, 16, 2], P('pipe', 'ctx'), may hold values from -1 to 15, as said below
- gain: float32 [2, 4096], P('pipe'), may hold values from 0.5 to 2
- w_router: bfloat16 [2, 4096], P('pipe'), may hold values from -0.09375 to 0.09375
- w_gate: bfloat16 [2, 14336, 4096], P('pipe', 'ctx'), may hold values from -0.09375 to 0.09375
- w_up: bfloat16 [2, 14336, 4096], P('pipe', 'ctx'), may hold values from -0.09375 to 0.09375
- w_down: bfloat16 [2, 14336, 4096], P('pipe', 'ctx'), may hold values from -0.046875 to 0.046875
Outputs:
- grad_inputs: bfloat16 [2, 2048, 4096], P('pipe', 'ctx')
- grad_gate: float32 [2, 14336, 4096], P('pipe', 'ctx')
- grad_up: float32 [2, 14336, 4096], P('pipe', 'ctx')
- grad_down: float32 [2, 14336, 4096], P('pipe', 'ctx')
- grad_gain: float32 [2, 4096], P('pipe')
- grad_router: float32 [2, 4096], P('pipe')
Inputs may be any that keep to these rules, and one draw needn't show every extreme that they name: In each row route_blocks[l, o, :] the 2 entries are distinct block numbers of owner o; only slots whose route_dest entry is not -1 are routed. In each row route_dest[l, o, :] the used slots come first: blocks that owner o works on itself (entry o), then blocks handed to the next owner (entry (o + 1) mod 16), then -1. An owner keeps at most 1 block and hands on at most 1; every device works on exactly 1 block of each layer, so 16 * 1 blocks are routed in each layer; in each layer some owner uses all 2 slots, keeping 1 and handing on 1.
All inputs are finite; a program needn't handle non-finite values.
Results may differ from a plain program's by a relative error of at most 0.007.
Values may be sent and summed in bfloat16 or wider, within the bound.
No kernel may reach another device: no remote copies, remote signals or barrier semaphores. Data moves between devices by JAX's collectives and lax.ppermute only.
A program may use at most 128 MiB of HBM per device.

v0:
```python
import functools

import jax
import jax.numpy as jnp
from jax import lax
from jax.experimental import pallas as pl
from jax.experimental.pallas import tpu as pltpu
from jax.sharding import PartitionSpec as P

BLOCK = 4
EPSILON = 1e-05
LANES = 128
CHUNK = 512
WIDE = 1024
SHARES = (7, 4, 4, 4, 2, 0)
GROUP = 16
TILE = 256
VMEM_LIMIT = 10 * 1024 * 1024
STREAM_LIMIT = 52 * 1024 * 1024
SMALL_LIMIT = 6 * 1024 * 1024

F32 = jnp.float32
BF16 = jnp.bfloat16
VMEM_SPEC = pl.BlockSpec(memory_space=pltpu.VMEM)
SMEM_SPEC = pl.BlockSpec(memory_space=pltpu.SMEM)
ANY_SPEC = pl.BlockSpec(memory_space=pl.ANY)
HBM_SPEC = pl.BlockSpec(memory_space=pltpu.HBM)


def hop_order(peers):
    masks = []
    step = 1
    while step < peers:
        masks.append(step)
        step *= 2
    return masks[2:] + masks[:2][::-1]


def exchange(block, mask):
    peers = lax.axis_size("ctx")
    return lax.ppermute(block, "ctx", [(i, i ^ mask) for i in range(peers)])


def first_pair(kept, handed, weight):
    peers = lax.axis_size("ctx")
    mask = hop_order(peers)[0]
    came = lax.ppermute(handed, "ctx", [(i, (i + 1) % peers) for i in range(peers)])
    far_kept = exchange(kept, mask)
    far_came = lax.ppermute(handed, "ctx", [(i, ((i + 1) % peers) ^ mask) for i in range(peers)])
    came, weight = beside(came, handed, weight)
    used = kept.shape[1] - LANES + 3
    mine = jnp.where(kept[:1, used : used + 1] > 0.5, kept, came)
    far = jnp.where(far_kept[:1, used : used + 1] > 0.5, far_kept, far_came)
    return mine, jnp.stack([mine, far]), weight


def gather_all(held, weights):
    masks = hop_order(lax.axis_size("ctx"))
    cut = (held.shape[2] - LANES) // 2
    up_w, down_w = weights
    for mask in masks[1:-2]:
        came = exchange(held, mask)
        if mask == masks[-3]:
            came, up_w = beside(came, held, up_w)
        held = jnp.concatenate([held, came], axis=0)
    near, far = masks[-2:]
    first, second = held[:, :, :cut], held[:, :, cut:]
    count = held.shape[0]
    first_near = exchange(first, near)
    second_far = exchange(second, far)
    second_far, down_w = beside(second_far, second, down_w)
    first = jnp.concatenate([first, first_near], axis=0)
    second_pair = jnp.concatenate([second, second_far], axis=0)
    first_far = exchange(first, far)
    second_near = exchange(second_pair, near)
    first = jnp.concatenate([first, first_far], axis=0)
    second = jnp.concatenate(
        [second, second_near[:count], second_far, second_near[count:]], axis=0
    )
    return (first, second), (up_w, down_w)


def scatter_sum(chunks, sent, stats, outers):
    rows = stats.shape[0]
    masks = hop_order(lax.axis_size("ctx"))[::-1]
    for step, mask in enumerate(masks):
        if step > 0:
            half = chunks.shape[0] // 2
            high = lax.reduce_precision(stats, 8, 7)
            both = jnp.concatenate([high, stats - high], axis=0).astype(BF16)
            sent = jnp.concatenate([chunks[half:].astype(BF16), both[None]], axis=0)
            chunks = chunks[:half]
        received = outers.beside(exchange(sent, mask), sent)
        if mask == masks[-1]:
            break
        received = received.astype(F32)
        half = chunks.shape[0]
        chunks = chunks + received[:half]
        stats = stats + received[half, :rows] + received[half, rows:]
    return chunks[0], stats, received


def sum_all(rows, weights):
    total = rows.astype(F32)
    fetched = []
    for mask in hop_order(lax.axis_size("ctx")):
        sent = total.astype(BF16)
        received = exchange(sent, mask)
        if len(fetched) < len(weights):
            received, weight = beside(received, sent, weights[len(fetched)])
            fetched.append(weight)
        total = total + received.astype(F32)
    return total, fetched


def contract_last(left_side, right_side):
    return lax.dot_general(
        left_side, right_side, (((1,), (1,)), ((), ())), preferred_element_type=F32
    )


def route_slots(blocks_ref, dest_ref, me):
    first, second = blocks_ref[0, 0, 0], blocks_ref[0, 0, 1]
    kept = dest_ref[0, 0, 0] == me
    handed = jnp.where(kept, dest_ref[0, 0, 1], dest_ref[0, 0, 0]) >= 0
    return (first, kept), (jnp.where(kept, second, first), handed)


def pick_kernel(
    here_ref, blocks_ref, dest_ref, other_blocks_ref, other_dest_ref, saved_ref, grad_ref,
    keep_ref, hand_ref, groups, sems,
):
    model_dim = saved_ref.shape[1]
    me = here_ref[1]
    slots = route_slots(blocks_ref, dest_ref, me)
    copies = []
    for slot, (block, _) in enumerate(slots):
        first = pl.multiple_of((block * BLOCK) // GROUP * GROUP, GROUP)
        for kind, source in enumerate((saved_ref, grad_ref)):
            copy = pltpu.make_async_copy(
                source.at[pl.ds(first, GROUP)], groups.at[slot, kind], sems.at[slot, kind]
            )
            copy.start()
            copies.append(copy)
    for copy in copies:
        copy.wait()
    rows = lax.broadcasted_iota(jnp.int32, (8, GROUP), 0)
    cols = lax.broadcasted_iota(jnp.int32, (8, GROUP), 1)
    lane = lax.broadcasted_iota(jnp.int32, (8, LANES), 1)
    for slot, out in enumerate((keep_ref, hand_ref)):
        block, used = slots[slot]
        offset = (block * BLOCK) % GROUP
        from_saved = jnp.where((rows < BLOCK) & (cols == offset + rows), 1.0, 0.0).astype(BF16)
        from_grad = jnp.where(
            (rows >= BLOCK) & (cols == offset + rows - BLOCK), 1.0, 0.0
        ).astype(BF16)
        for start in range(0, model_dim, CHUNK):
            at = slice(start, start + CHUNK)
            picked = jnp.dot(
                from_saved, groups[slot, 0, :, at], preferred_element_type=F32
            ) + jnp.dot(from_grad, groups[slot, 1, :, at], preferred_element_type=F32)
            out[:, at] = picked.astype(BF16)
        shared = jnp.int32(0)
        for j in range(2):
            same = (other_blocks_ref[0, 0, j] == block) & (other_dest_ref[0, 0, j] >= 0)
            shared = jnp.where(same & used, 1, shared)
        meta = jnp.zeros((8, LANES), F32)
        for index, value in enumerate((me, block, shared, used.astype(jnp.int32))):
            meta = jnp.where(lane == index, value.astype(F32), meta)
        out[:, model_dim:] = meta.astype(BF16)


def pick_blocks(here, routes, saved, grad):
    model_dim = saved.shape[1]
    shape = jax.ShapeDtypeStruct((8, model_dim + LANES), BF16)
    return pl.pallas_call(
        pick_kernel,
        out_shape=(shape, shape),
        in_specs=[SMEM_SPEC] * 5 + [ANY_SPEC, ANY_SPEC],
        out_specs=(VMEM_SPEC, VMEM_SPEC),
        scratch_shapes=[
            pltpu.VMEM((2, 2, GROUP, model_dim), BF16),
            pltpu.SemaphoreType.DMA((2, 2)),
        ],
        compiler_params=pltpu.CompilerParams(vmem_limit_bytes=SMALL_LIMIT),
    )(here, *routes, *(pltpu.with_memory_space_constraint(a, pltpu.HBM) for a in (saved, grad)))


def layer_kernel(with_delta, stream, tile, *refs):
    if with_delta:
        delta_ref, active_ref, up_slope_ref, hidden_ref = refs[:4]
        refs = refs[4:]
    here_ref, first_ref, second_ref, gain_ref, router_ref, gate_w, up_w, down_w = refs[:8]
    refs = refs[8:]
    gate_grad_ref, up_grad_ref, scaled_ref, keep_ref, sent_ref, stat_ref = refs[:6]
    refs = refs[6:]
    if not with_delta:
        hidden_ref, normed_ref, active_ref, up_slope_ref = refs[:4]
        shared_part_ref, shared_x_ref, case_ref = refs[4:7]
        refs = refs[7:]
    picked_s, up_s = refs[:2]
    waits = ()
    if stream:
        *held, sems = refs[2:]
        copies = [
            pltpu.make_async_copy(source, target, sems.at[index])
            for index, (source, target) in enumerate(zip((down_w, gate_w, up_w), held))
        ]
        for copy in copies:
            copy.start()
        down_w, gate_w, up_w = held
        waits = (copies[:1], copies[1:]) if with_delta else (copies, ())
    half_pairs = first_ref.shape[0]
    quarter = half_pairs // 2
    rows = half_pairs * 8
    model_dim = scaled_ref.shape[1]
    ff_local = gate_grad_ref.shape[1]
    middle = model_dim // 2

    def split(ref, start, width):
        even = ref[:, 0, :, pl.ds(start, width)].astype(F32)
        odd = ref[:, 1, :, pl.ds(start, width)].astype(F32)
        low = lax.broadcasted_iota(jnp.int32, even.shape, 1) < BLOCK
        first = jnp.where(low, even, pltpu.roll(odd, BLOCK, 1)).reshape(rows, width)
        second = jnp.where(low, pltpu.roll(even, BLOCK, 1), odd).reshape(rows, width)
        return first, second

    def gather_chunk(c, carry):
        squares, logits = carry
        inner = pl.multiple_of(c * WIDE, WIDE)
        for ref, base in ((first_ref, 0), (second_ref, middle)):
            at = pl.ds(pl.multiple_of(inner + base, WIDE), WIDE)
            x, g = split(ref, inner, WIDE)
            picked_s[:, at] = x.astype(BF16)
            up_s[:, at] = g.astype(BF16)
            squares = squares + jnp.sum(x * x, axis=1, keepdims=True)
            logits = logits + jnp.sum(x * router_ref[:, at].astype(F32), axis=1, keepdims=True)
        return squares, logits

    zero = jnp.zeros((rows, 1), F32)
    squares, logits = lax.fori_loop(0, middle // WIDE, gather_chunk, (zero, zero))
    inverse = lax.rsqrt(squares * (1.0 / model_dim) + EPSILON)
    router = jax.nn.sigmoid(logits)

    meta, _ = split(second_ref, middle, LANES)
    lane = lax.broadcasted_iota(jnp.int32, (8, LANES), 1)
    pick = lax.broadcasted_iota(jnp.int32, (8, LANES), 0) == lane
    across = contract_last(jnp.where(pick, 1.0, 0.0).astype(BF16), meta.astype(BF16))
    key_row = across[0:1] * LANES + across[1:2]
    key_col = meta[:, 0:1] * LANES + meta[:, 1:2]
    row_a = lax.broadcasted_iota(jnp.int32, (rows, rows), 0)
    row_b = lax.broadcasted_iota(jnp.int32, (rows, rows), 1)
    ahead = (key_col < key_row) & (meta[:, 2:3] > 0.5) & (row_a % BLOCK == 0)
    rank = jnp.sum(jnp.where(ahead, 1.0, 0.0), axis=0, keepdims=True)
    place = rank.astype(jnp.int32) * BLOCK + row_b % BLOCK
    chosen = jnp.where((place == row_a) & (across[2:3] > 0.5), 1.0, 0.0).astype(BF16)
    if with_delta:
        lower = jnp.where(here_ref[0] == 0, 1.0, 0.0).astype(BF16)
        spread = chosen[: delta_ref.shape[0]] * lower
    else:
        blocks = jnp.sum(across[2:3]) * (1.0 / BLOCK)
        few = shared_x_ref.shape[0] // BLOCK
        case_ref[0] = jnp.where(blocks > few + 0.5, 2, jnp.where(blocks > 0.5, 1, 0))
        chosen = chosen[: shared_x_ref.shape[0]]

    def scale_chunk(c, carry):
        at = pl.ds(pl.multiple_of(c * WIDE, WIDE), WIDE)
        x = picked_s[:, at]
        upstream = up_s[:, at].astype(F32)
        if with_delta:
            added = lax.dot_general(
                spread, delta_ref[:, at], (((0,), (0,)), ((), ())), preferred_element_type=F32
            )
            upstream = (upstream + added).astype(BF16).astype(F32)
        else:
            normed_ref[:, at] = (x.astype(F32) * inverse * gain_ref[:, at]).astype(BF16)
            shared_x_ref[:, at] = jnp.dot(chosen, x, preferred_element_type=F32).astype(BF16)
        scaled_ref[:, at] = (router * upstream).astype(BF16)
        return carry

    lax.fori_loop(0, model_dim // WIDE, scale_chunk, 0)

    row_sums = zero
    for copy in waits[0] if stream else ():
        copy.wait()
    for begin in range(0, ff_local, tile):
        at = slice(begin, min(begin + tile, ff_local))
        hidden_grad = contract_last(down_w[at, :], scaled_ref[...])
        if with_delta:
            activated = active_ref[at, :]
            up_slope = up_slope_ref[at, :]
        else:
            gate = contract_last(gate_w[at, :], normed_ref[...])
            up = contract_last(up_w[at, :], normed_ref[...])
            sigma = jax.nn.sigmoid(gate)
            activated = gate * sigma
            up_slope = up * (sigma * (1.0 + gate * (1.0 - sigma)))
            hidden = (activated * up).astype(BF16)
            hidden_ref[:, at] = hidden.T
            active_ref[at, :] = activated
            up_slope_ref[at, :] = up_slope
        gate_grad_ref[:, at] = (hidden_grad * up_slope).astype(BF16).T
        up_grad_ref[:, at] = (hidden_grad * activated).astype(BF16).T
        if with_delta:
            hidden = hidden_ref[:, at].T
        row_sums = row_sums + jnp.sum(hidden_grad * hidden.astype(F32), axis=0, keepdims=True).T
    logit_part = row_sums * (1.0 - router)

    low = lax.broadcasted_iota(jnp.int32, (half_pairs, 8, 1), 1) < BLOCK

    def store(even, odd, at):
        keep_ref[:, 0, :, at] = even[:quarter]
        keep_ref[:, 1, :, at] = odd[:quarter]
        for q in range(quarter):
            sent_ref[2 * q, :, at] = even[quarter + q].astype(BF16)
            sent_ref[2 * q + 1, :, at] = odd[quarter + q].astype(BF16)

    for copy in waits[1] if stream else ():
        copy.wait()

    def out_chunk(c, carry):
        at = pl.ds(pl.multiple_of(c * WIDE, WIDE), WIDE)
        halves = []
        gains = []
        routers = []
        for second in range(2):
            cols = pl.ds(pl.multiple_of(c * WIDE + second * middle, WIDE), WIDE)
            grad = jnp.dot(
                gate_grad_ref[...], gate_w[:, cols], preferred_element_type=F32
            ) + jnp.dot(up_grad_ref[...], up_w[:, cols], preferred_element_type=F32)
            x = picked_s[:, cols].astype(F32)
            gains.append(jnp.sum(grad * (x * inverse), axis=0, keepdims=True))
            routers.append(jnp.sum(logit_part * x, axis=0, keepdims=True))
            if not with_delta:
                shared_part_ref[:, cols] = jnp.dot(
                    chosen, grad.astype(BF16), preferred_element_type=F32
                ).astype(BF16)
            halves.append(grad.reshape(half_pairs, 8, WIDE))
        a, b = halves
        store(
            jnp.where(low, a, pltpu.roll(b, BLOCK, 1)),
            jnp.where(low, pltpu.roll(a, BLOCK, 1), b),
            at,
        )
        stats = jnp.concatenate(gains + routers, axis=0)
        high = stats.astype(BF16).astype(F32)
        stat_ref[:, at] = stats
        sent_ref[2 * quarter, :, at] = jnp.concatenate([high, stats - high], axis=0).astype(BF16)
        return carry

    lax.fori_loop(0, middle // WIDE, out_chunk, 0)
    wide = jnp.broadcast_to(row_sums, (rows, LANES))
    if not with_delta:
        shared_part_ref[:, model_dim:] = jnp.dot(
            chosen, wide.astype(BF16), preferred_element_type=F32
        ).astype(BF16)
    wide = wide.reshape(half_pairs, 8, LANES)
    store(wide, pltpu.roll(wide, BLOCK, 1), pl.ds(middle, LANES))
    stat_ref[:, middle:] = jnp.zeros((4, LANES), F32)
    sent_ref[2 * quarter, :, middle:] = jnp.zeros((8, LANES), BF16)


def fetch_kernel(source_ref, out_ref, sems):
    parts = sems.shape[0]
    size = source_ref.shape[0] // parts
    copies = []
    for part in range(parts):
        at = pl.ds(part * size, size)
        copy = pltpu.make_async_copy(source_ref.at[at], out_ref.at[at], sems.at[part])
        copy.start()
        copies.append(copy)
    for copy in copies:
        copy.wait()


def fetch(weight):
    return pl.pallas_call(
        fetch_kernel,
        out_shape=pltpu.VMEM(weight.shape, weight.dtype),
        in_specs=[HBM_SPEC],
        out_specs=VMEM_SPEC,
        scratch_shapes=[pltpu.SemaphoreType.DMA((7,))],
        compiler_params=pltpu.CompilerParams(vmem_limit_bytes=8 * 1024 * 1024),
        cost_estimate=pl.CostEstimate(
            flops=0, bytes_accessed=2 * weight.size, transcendentals=0
        ),
    )(pltpu.with_memory_space_constraint(weight, pltpu.HBM))


def beside(received, sent, weight):
    weight, _ = lax.optimization_barrier((weight, sent))
    fetched = fetch(weight)
    received, fetched = lax.optimization_barrier((received, fetched))
    return received, fetched


def layer_pass(here, pay, gain, router, weights, few, again=None, stream=False):
    peers = pay[0].shape[0]
    rows = peers * BLOCK
    ff_local, model_dim = weights[0].shape
    wide = model_dim // 2 + LANES
    pairs = [part.reshape((peers // 2, 2) + part.shape[1:]) for part in pay]
    if not stream:
        weights = [pltpu.with_memory_space_constraint(w, pltpu.VMEM) for w in weights]
    operands = [here, *pairs, gain, router, *weights]
    in_specs = [SMEM_SPEC] + [VMEM_SPEC] * 4 + [ANY_SPEC if stream else VMEM_SPEC] * 3
    scratch = [pltpu.VMEM((rows, model_dim), BF16)] * 2
    if stream:
        scratch += [pltpu.VMEM((ff_local, model_dim), BF16)] * 3
        scratch += [pltpu.SemaphoreType.DMA((3,))]
    small = jax.ShapeDtypeStruct((rows, ff_local), BF16)
    large = jax.ShapeDtypeStruct((rows, model_dim), BF16)
    tall = jax.ShapeDtypeStruct((ff_local, rows), F32)
    out_shape = [
        small,
        small,
        large,
        jax.ShapeDtypeStruct((peers // 4, 2, 8, wide), F32),
        jax.ShapeDtypeStruct((peers // 2 + 1, 8, wide), BF16),
        jax.ShapeDtypeStruct((4, wide), F32),
    ]
    out_specs = [VMEM_SPEC] * len(out_shape)
    if again is None:
        out_shape += [
            small,
            large,
            tall,
            tall,
            jax.ShapeDtypeStruct((few, model_dim + LANES), BF16),
            jax.ShapeDtypeStruct((few, model_dim), BF16),
            jax.ShapeDtypeStruct((1,), jnp.int32),
        ]
        out_specs += [VMEM_SPEC] * 6 + [SMEM_SPEC]
    else:
        operands = [*again, *operands]
        in_specs = [VMEM_SPEC] * len(again) + in_specs
    outs = pl.pallas_call(
        functools.partial(layer_kernel, again is not None, stream, TILE),
        out_shape=out_shape,
        in_specs=in_specs,
        out_specs=out_specs,
        scratch_shapes=scratch,
        compiler_params=pltpu.CompilerParams(
            vmem_limit_bytes=STREAM_LIMIT if stream else VMEM_LIMIT * max(1, rows // 64)
        ),
        cost_estimate=pl.CostEstimate(
            flops=10 * rows * ff_local * model_dim,
            bytes_accessed=6 * ff_local * model_dim,
            transcendentals=rows * ff_local,
        ),
    )(*operands)
    return tuple(outs[:6]), tuple(outs[6:])


def outer_kernel(tile, first, count, left_ref, right_ref, *refs):
    out_ref, ring, sems = refs[-3:]
    depth = ring.shape[0]
    copies = []
    for t in range(count):
        slot = t % depth
        if t >= depth:
            copies[t - depth].wait()
        ring[slot] = lax.dot_general(
            left_ref[:, (first + t) * tile : (first + t + 1) * tile],
            right_ref[...],
            (((0,), (0,)), ((), ())),
            preferred_element_type=F32,
        )
        copy = pltpu.make_async_copy(
            ring.at[slot], out_ref.at[pl.ds((first + t) * tile, tile)], sems.at[slot]
        )
        copy.start()
        copies.append(copy)
    for copy in copies[-depth:]:
        copy.wait()


def outer_tile(ff_local):
    return LANES if ff_local % LANES == 0 else ff_local


def weight_grad(left, right, first, count, into):
    rows, ff_local = left.shape
    model_dim = right.shape[1]
    tile = outer_tile(ff_local)
    depth = min(4, count)
    operands = [left, right] + ([] if into is None else [into])
    return pl.pallas_call(
        functools.partial(outer_kernel, tile, first, count),
        out_shape=jax.ShapeDtypeStruct((ff_local, model_dim), F32),
        in_specs=[VMEM_SPEC, VMEM_SPEC, ANY_SPEC][: len(operands)],
        out_specs=ANY_SPEC,
        input_output_aliases={} if into is None else {2: 0},
        scratch_shapes=[
            pltpu.VMEM((depth, tile, model_dim), F32),
            pltpu.SemaphoreType.DMA((depth,)),
        ],
        compiler_params=pltpu.CompilerParams(vmem_limit_bytes=16 * 1024 * 1024),
        cost_estimate=pl.CostEstimate(
            flops=2 * rows * count * tile * model_dim,
            bytes_accessed=4 * count * tile * model_dim,
            transcendentals=0,
        ),
    )(*operands)


class Outers:
    def __init__(self, factors, windows):
        tiles = factors[0][0].shape[1] // outer_tile(factors[0][0].shape[1])
        self.factors = factors
        self.results = [None] * len(factors)
        total = tiles * len(factors)
        shares = SHARES if windows == len(SHARES) else (1,) * windows
        ends = [total * sum(shares[: i + 1]) // sum(shares) for i in range(windows)]
        self.pieces = []
        for begin, end in zip([0] + ends[:-1], ends):
            piece = []
            while begin < end:
                which, first = divmod(begin, tiles)
                count = min(end - begin, tiles - first)
                piece.append((which, first, count))
                begin += count
            self.pieces.append(piece)

    def beside(self, received, sent):
        for which, first, count in self.pieces.pop(0):
            left, right = self.factors[which]
            left, _ = lax.optimization_barrier((left, sent))
            result = weight_grad(left, right, first, count, self.results[which])
            received, self.results[which] = lax.optimization_barrier((received, result))
        return received


def norm_backward(x, grad, row_sum, gain, weight):
    inverse = lax.rsqrt(jnp.mean(x * x, axis=1, keepdims=True) + EPSILON)
    hat = x * inverse
    router = jax.nn.sigmoid(jnp.sum(x * weight, axis=1, keepdims=True))
    hat_grad = grad * gain
    norm_part = inverse * (hat_grad - hat * jnp.mean(hat_grad * hat, axis=1, keepdims=True))
    return norm_part + row_sum * (1.0 - router) * weight


def delta_kernel(
    pay_ref, sum_ref, stat_ref, last_ref, gain_ref, router_ref, out_ref, gain_out_ref, router_out_ref
):
    middle = out_ref.shape[1]
    x = pay_ref[...].astype(F32)[:BLOCK, : 2 * middle]
    sums = sum_ref[...] + last_ref[0].astype(F32)
    far = last_ref[1].astype(F32)
    stats = stat_ref[...] + far[:BLOCK] + far[BLOCK:]
    grad = jnp.concatenate([sums[:BLOCK, :middle], sums[BLOCK:, :middle]], axis=1)
    row_sum = sums[:BLOCK, middle : middle + 1]
    delta = norm_backward(x, grad, row_sum, gain_ref[...], router_ref[...].astype(F32))
    out_ref[...] = jnp.concatenate([delta[:, :middle], delta[:, middle:]], axis=0).astype(BF16)
    for second in range(2):
        cols = slice(second * middle, (second + 1) * middle)
        gain_out_ref[:, cols] = stats[second : second + 1, :middle]
        router_out_ref[:, cols] = stats[2 + second : 3 + second, :middle]


def delta_rows(pay, sums, stats, last, gain, router):
    row = jax.ShapeDtypeStruct(gain.shape, F32)
    return pl.pallas_call(
        delta_kernel,
        out_shape=(jax.ShapeDtypeStruct((8, sums.shape[1] - LANES), BF16), row, row),
        in_specs=[VMEM_SPEC] * 6,
        out_specs=(VMEM_SPEC,) * 3,
        compiler_params=pltpu.CompilerParams(vmem_limit_bytes=SMALL_LIMIT),
    )(pay, sums, stats, last, gain, router)


def shared_kernel(x_ref, sum_ref, gain_ref, router_ref, out_ref):
    model_dim = x_ref.shape[1]
    delta = norm_backward(
        x_ref[...].astype(F32),
        sum_ref[:, :model_dim],
        sum_ref[:, model_dim : model_dim + 1],
        gain_ref[...],
        router_ref[...].astype(F32),
    )
    out_ref[...] = delta.astype(BF16)


def shared_rows(x, sums, gain, router):
    return pl.pallas_call(
        shared_kernel,
        out_shape=jax.ShapeDtypeStruct(x.shape, BF16),
        in_specs=[VMEM_SPEC] * 4,
        out_specs=VMEM_SPEC,
        compiler_params=pltpu.CompilerParams(
            vmem_limit_bytes=(4 if x.shape[0] <= 8 else 28) * 1024 * 1024
        ),
    )(x, sums, gain, router)


def add_kernel(
    here_ref, blocks_ref, dest_ref, other_blocks_ref, other_dest_ref,
    own_ref, back_ref, other_ref, other_back_ref, grad_ref, out_ref,
):
    middle = own_ref.shape[1]
    lower = here_ref[0] == 0
    mine = route_slots(blocks_ref, dest_ref, here_ref[1])
    theirs = route_slots(other_blocks_ref, other_dest_ref, here_ref[1])
    out_ref[...] = grad_ref[...]
    row = lax.broadcasted_iota(jnp.int32, (GROUP, 1), 0)

    def add(block, used, deltas):
        at = pl.ds(pl.multiple_of((block * BLOCK) // GROUP * GROUP, GROUP), GROUP)
        mask = (row // BLOCK == block % (GROUP // BLOCK)) & used
        for half in range(2):
            cols = slice(half * middle, (half + 1) * middle)
            four = deltas[half * BLOCK : (half + 1) * BLOCK, :]
            spread = jnp.concatenate([four] * (GROUP // BLOCK), axis=0)
            out_ref[at, cols] = (
                out_ref[at, cols].astype(F32) + jnp.where(mask, spread, 0.0)
            ).astype(BF16)

    for slot, (own, other) in enumerate(((own_ref, other_ref), (back_ref, other_back_ref))):
        block = jnp.where(lower, theirs[slot][0], mine[slot][0])
        used = jnp.where(lower, theirs[slot][1], mine[slot][1])
        deltas = jnp.where(lower, other[...].astype(F32), own[...].astype(F32))
        add(block, used, deltas)
    for slot, own in enumerate((own_ref, back_ref)):
        add(mine[slot][0], mine[slot][1] & lower, own[...].astype(F32))


def add_rows(here, routes, deltas, grad):
    return pl.pallas_call(
        add_kernel,
        out_shape=jax.ShapeDtypeStruct(grad.shape, BF16),
        in_specs=[SMEM_SPEC] * 5 + [VMEM_SPEC] * 5,
        out_specs=VMEM_SPEC,
        compiler_params=pltpu.CompilerParams(vmem_limit_bytes=SMALL_LIMIT),
    )(here, *routes, *deltas, grad)


def on_device(saved, grad_out, route_blocks, route_dest, gain, w_router, w_gate, w_up, w_down):
    sections = lax.axis_size("pipe")
    peers = lax.axis_size("ctx")
    here = jnp.stack([lax.axis_index("pipe"), lax.axis_index("ctx")]).astype(jnp.int32)
    tokens = saved[0]
    model_dim = tokens.shape[1]

    swap = [(i, sections - 1 - i) for i in range(sections)]
    routes = (
        route_blocks,
        route_dest,
        lax.ppermute(route_blocks, "pipe", swap),
        lax.ppermute(route_dest, "pipe", swap),
    )
    kept_rows, handed_rows = pick_blocks(here, routes, tokens, grad_out)
    pay_mine, pair, gate_w = first_pair(kept_rows, handed_rows, w_gate[0])
    pay, (up_w, down_w) = gather_all(pair, (w_up[0], w_down[0]))
    few = 2 * BLOCK
    run = functools.partial(layer_pass, here, pay, gain, w_router)
    state, saved_parts = run((gate_w, up_w, down_w), few)
    hidden, normed, active, up_slope, shared_part, shared_x, case = saved_parts

    def corrected(count):
        def branch(state):
            weights = (w_gate[0], w_up[0], w_down[0])
            small = count == few
            if small:
                part, x = shared_part, shared_x
            else:
                part, x = run(weights, count, stream=True)[1][4:6]
            sums, fetched = sum_all(part, weights if small else ())
            upper = shared_rows(x, sums, gain, w_router)
            upper = lax.ppermute(upper, "pipe", swap)
            again = (upper, active, up_slope, hidden)
            return run(fetched if small else weights, few, again, stream=not small)[0]

        return branch

    state = lax.switch(
        case[0], (lambda state: state, corrected(few), corrected(peers * BLOCK)), state
    )
    gate_grad, up_grad, scaled, keep, sent, stats = state

    outers = Outers(
        ((hidden, scaled), (gate_grad, normed), (up_grad, normed)), len(hop_order(peers)) + 2
    )
    keep = keep.reshape((peers // 2,) + keep.shape[2:])
    sums, stats, last = scatter_sum(keep, sent, stats, outers)
    delta, grad_gain, grad_router = delta_rows(pay_mine, sums, stats, last, gain, w_router)
    back = lax.ppermute(delta, "ctx", [(i, (i - 1) % peers) for i in range(peers)])
    other = lax.ppermute(delta, "pipe", swap)
    back = outers.beside(back, delta)
    other_back = outers.beside(lax.ppermute(back, "pipe", swap), back)
    grad_inputs = add_rows(here, routes, (delta, back, other, other_back), grad_out)
    grad_down, grad_gate, grad_up = outers.results
    return (
        grad_inputs[None],
        grad_gate[None],
        grad_up[None],
        grad_down[None],
        grad_gain,
        grad_router,
    )


def solution(mesh):
    split = P("pipe", "ctx", None)
    row = P("pipe", None)
    return jax.shard_map(
        on_device,
        mesh=mesh,
        in_specs=(split, P("ctx", None), split, split, row, row, split, split, split),
        out_specs=(split, split, split, split, row, row),
        check_vma=False,
    )
```

profile of v0, /device:TPU:0, one launch (start us, length us, event | category | flops | bytes accessed | tf_op | source)
XLA Modules:
  0.0 121.0 jit_solution(1931014475180738370)
XLA Ops:
  3.7 2.1 %shard_map.136 = (bf16[8,4224]{1,0:T(8,128)(2,1)S(1)}, bf16[8,4224]{1,0:T(8,128)(2,1)S(1)}) custom-call(s32[2]{0:T(128)} %pad_add_fusion.here_ref.refs_0_, s32[1,1,2]{2,1,0:T(1,128)S(1)} %copy-done.2, s32[1,1,2]{2,1,0:T(1,128)S(1)} %copy-done.4, s32[1,1,2]{2,1,0:T(1,128)S(1)} %collective-permute-done.10.other_blocks_ref, ...), custom_call_target="tpu_custom_call" | custom-call | tf_op jit(solution)/shard_map/pallas_call | solution.py:176
  5.8 2.7 %collective-permute-start.12 = (bf16[8,4224]{1,0:T(8,128)(2,1)S(1)}, bf16[8,4224]{1,0:T(8,128)(2,1)S(1)}, u32[]{:S(2)}, u32[]{:S(2)}) collective-permute-start(bf16[8,4224]{1,0:T(8,128)(2,1)S(1)} %get-tuple-element.190), channel_id=1, source_target_pairs={{0,1},{1,2},{2,3},{3,4},{4,5},{5,6},{6,7},{7,8},{8,9},{9,10},{10,1... | collective-permute-start | bytes 202760 | tf_op jit(solution)/shard_map/ppermute | solution.py:47
  12.1 3.2 %shard_map.137.refs_5_ = bf16[896,4096]{1,0:T(8,128)(2,1)S(1)} custom-call(bf16[896,4096]{1,0:T(8,128)(2,1)} %bitcast.84), custom_call_target="tpu_custom_call" | custom-call | bytes 7340032 | tf_op jit(solution)/shard_map/pallas_call | solution.py:377
  17.3 2.7 %collective-permute-start.15 = (bf16[2,8,4224]{2,1,0:T(8,128)(2,1)S(1)}, bf16[2,8,4224]{2,1,0:T(8,128)(2,1)S(1)}, u32[]{:S(2)}, u32[]{:S(2)}) collective-permute-start(bf16[2,8,4224]{2,1,0:T(8,128)(2,1)S(1)} %pad_maximum_fusion.6), channel_id=1, source_target_pairs={{0,8},{1,9},{2,10},{3,11},{4,12},{5,13},{6,14},{7,15},{8,0},{9,1},... | collective-permute-start | bytes 405512 | tf_op jit(solution)/shard_map/ppermute | solution.py:41
  19.9 3.2 %shard_map.138.refs_6_ = bf16[896,4096]{1,0:T(8,128)(2,1)S(1)} custom-call(bf16[896,4096]{1,0:T(8,128)(2,1)} %bitcast.88), custom_call_target="tpu_custom_call" | custom-call | bytes 7340032 | tf_op jit(solution)/shard_map/pallas_call | solution.py:377
  23.1 3.0 %collective-permute-done.15 = bf16[2,8,4224]{2,1,0:T(8,128)(2,1)S(1)} collective-permute-done((bf16[2,8,4224]{2,1,0:T(8,128)(2,1)S(1)}, bf16[2,8,4224]{2,1,0:T(8,128)(2,1)S(1)}, u32[]{:S(2)}, u32[]{:S(2)}) %collective-permute-start.15) | collective-permute-done | bytes 135200 | tf_op jit(solution)/shard_map/ppermute | solution.py:41
  28.4 3.2 %shard_map.139.refs_7_ = bf16[896,4096]{1,0:T(8,128)(2,1)S(1)} custom-call(bf16[896,4096]{1,0:T(8,128)(2,1)} %bitcast.92), custom_call_target="tpu_custom_call" | custom-call | bytes 7340032 | tf_op jit(solution)/shard_map/pallas_call | solution.py:377
  33.7 4.7 %collective-permute-done.17 = bf16[8,8,2048]{2,1,0:T(8,128)(2,1)S(1)} collective-permute-done((bf16[8,8,2048]{2,1,0:T(8,128)(2,1)S(1)}, bf16[8,8,2048]{2,1,0:T(8,128)(2,1)S(1)}, u32[]{:S(2)}, u32[]{:S(2)}) %collective-permute-start.17) | collective-permute-done | bytes 262176 | tf_op jit(solution)/shard_map/ppermute | solution.py:41
  40.1 12.5 %shard_map.140 = (bf16[64,896]{1,0:T(8,128)(2,1)}, bf16[64,896]{1,0:T(8,128)(2,1)S(1)}, bf16[64,4096]{1,0:T(8,128)(2,1)}, f32[4,2,8,2176]{3,2,1,0:T(8,128)S(1)},...) custom-call(s32[2]{0:T(128)} %pad_add_fusion.here_ref.refs_0_, ...), custom_call_target="tpu_custom_call" | custom-call | flops 2348810240 | bytes 22020096 | tf_op jit(solution)/shard_map/pallas_call | solution.py:437
  53.3 30.0 %conditional.1 = ((bf16[64,896]{1,0:T(8,128)(2,1)}, bf16[64,896]{1,0:T(8,128)(2,1)S(1)}, bf16[64,4096]{1,0:T(8,128)(2,1)}, bf16[9,8,2176]{2,1,0:T(8,128)(2,1)}, ...) conditional(s32[]{:T(128)} %bitcast.22, (bf16[64,896]{1,0:T(8,128)(2,1)}, ...), branch_computations={%region_0.1_spmd, %region_1.2_spmd, %region_2.3_spmd} | conditional | flops 4704919552 | bytes 98681168 | solution.py:675
  54.8 3.2 %branch_1_fun.5.refs_9_ = bf16[896,4096]{1,0:T(8,128)(2,1)S(1)} custom-call(bf16[896,4096]{1,0:T(8,128)(2,1)} %bitcast.85), custom_call_target="tpu_custom_call" | custom-call | bytes 7340032 | tf_op jit(solution)/shard_map/cond/branch_1_fun/pallas_call | solution.py:377
  58.0 3.5 %collective-permute-start.1 = (bf16[8,4224]{1,0:T(8,128)(2,1)S(1)}, bf16[8,4224]{1,0:T(8,128)(2,1)S(1)}, u32[]{:S(2)}, u32[]{:S(2)}) collective-permute-start(bf16[8,4224]{1,0:T(8,128)(2,1)S(1)} %fusion), channel_id=1, source_target_pairs={{0,8},{1,9},{2,10},{3,11},{4,12},{5,13},{6,14},{7,15},{8,0},{9,1},... | collective-permute-start | bytes 202760 | tf_op jit(solution)/shard_map/cond/branch_1_fun/ppermute | solution.py:41
  61.5 3.2 %branch_1_fun.6.refs_10_ = bf16[896,4096]{1,0:T(8,128)(2,1)S(1)} custom-call(bf16[896,4096]{1,0:T(8,128)(2,1)} %bitcast.89), custom_call_target="tpu_custom_call" | custom-call | bytes 7340032 | tf_op jit(solution)/shard_map/cond/branch_1_fun/pallas_call | solution.py:377
  65.4 3.2 %branch_1_fun.7.refs_11_ = bf16[896,4096]{1,0:T(8,128)(2,1)S(1)} custom-call(bf16[896,4096]{1,0:T(8,128)(2,1)} %bitcast.93), custom_call_target="tpu_custom_call" | custom-call | bytes 7340032 | tf_op jit(solution)/shard_map/cond/branch_1_fun/pallas_call | solution.py:377
  70.2 3.2 %collective-permute-done.3 = bf16[8,4224]{1,0:T(8,128)(2,1)S(1)} collective-permute-done((bf16[8,4224]{1,0:T(8,128)(2,1)S(1)}, bf16[8,4224]{1,0:T(8,128)(2,1)S(1)}, u32[]{:S(2)}, u32[]{:S(2)}) %collective-permute-start.3) | collective-permute-done | bytes 67616 | tf_op jit(solution)/shard_map/cond/branch_1_fun/ppermute | solution.py:41
  75.1 8.2 %branch_1_fun.9 = (bf16[64,896]{1,0:T(8,128)(2,1)}, bf16[64,896]{1,0:T(8,128)(2,1)S(1)}, bf16[64,4096]{1,0:T(8,128)(2,1)}, f32[4,2,8,2176]{3,2,1,0:T(8,128)S(1)}...) custom-call(bf16[8,4096]{1,0:T(8,128)(2,1)S(1)} %collective-permute-done.4.refs_0_, ...), custom_call_target="tpu_custom_call" | custom-call | flops 2348810240 | bytes 22020096 | tf_op jit(solution)/shard_map/cond/branch_1_fun/pallas_call | solution.py:437
  84.3 6.7 %shard_map.141 = f32[896,4096]{1,0:T(8,128)} custom-call(bf16[64,896]{1,0:T(8,128)(2,1)S(1)} %get-tuple-element.214.left_ref, bf16[64,4096]{1,0:T(8,128)(2,1)} %get-tuple-element.249.right_ref), custom_call_target="tpu_custom_call" | custom-call | flops 469762048 | bytes 14680064 | tf_op jit(solution)/shard_map/pallas_call | solution.py:488
  94.2 3.8 %shard_map.142.refs_0_ = f32[896,4096]{1,0:T(8,128)} custom-call(bf16[64,896]{1,0:T(8,128)(2,1)S(1)} %copy-done.10, bf16[64,4096]{1,0:T(8,128)(2,1)S(1)} %get-tuple-element.220.right_ref), custom_call_target="tpu_custom_call" | custom-call | flops 268435456 | bytes 8388608 | tf_op jit(solution)/shard_map/pallas_call | solution.py:488
  99.0 2.2 %collective-permute-start.22 = (bf16[3,8,2176]{2,1,0:T(8,128)(2,1)S(1)}, bf16[3,8,2176]{2,1,0:T(8,128)(2,1)S(1)}, u32[]{:S(2)}, u32[]{:S(2)}) collective-permute-start(bf16[3,8,2176]{2,1,0:T(8,128)(2,1)S(1)} %maximum_maximum_fusion.1), channel_id=1, source_target_pairs={{0,8},{1,9},{2,10},{3,11},{4,12},{5,13},{6,14},{7,15},{8,0},{9,1},... | collective-permute-start | bytes 313352 | tf_op jit(solution)/shard_map/ppermute | solution.py:41
  103.0 3.2 %shard_map.143 = f32[896,4096]{1,0:T(8,128)} custom-call(bf16[64,896]{1,0:T(8,128)(2,1)S(1)} %copy-done.10, bf16[64,4096]{1,0:T(8,128)(2,1)S(1)} %get-tuple-element.220.right_ref, f32[896,4096]{1,0:T(8,128)} %shard_map.142.refs_0_), custom_call_target="tpu_custom_call", output_to_operand_aliasing={{}: (2, {})} | custom-call | flops 201326592 | bytes 6291456 | tf_op jit(solution)/shard_map/pallas_call | solution.py:488
  108.1 3.8 %shard_map.145.refs_0_ = f32[896,4096]{1,0:T(8,128)} custom-call(bf16[64,896]{1,0:T(8,128)(2,1)S(1)} %get-tuple-element.232.left_ref, bf16[64,4096]{1,0:T(8,128)(2,1)S(1)} %get-tuple-element.220.right_ref, f32[896,4096]{1,0:T(8,128)} %shard_map.144.refs_0_), custom_call_target="tpu_custom_call", output_to_operand_aliasing={{}: (2, {})} | custom-call | flops 268435456 | bytes 8388608 | tf_op jit(solution)/shard_map/pallas_call | solution.py:488
  112.8 2.4 %collective-permute-start.24 = (bf16[8,2048]{1,0:T(8,128)(2,1)S(1)}, bf16[8,2048]{1,0:T(8,128)(2,1)S(1)}, u32[]{:S(2)}, u32[]{:S(2)}) collective-permute-start(bf16[8,2048]{1,0:T(8,128)(2,1)S(1)} %get-tuple-element.231.own_ref), channel_id=1, source_target_pairs={{0,15},{1,0},{2,1},{3,2},{4,3},{5,4},{6,5},{7,6},{8,7},{9,8},{10,9... | collective-permute-start | bytes 98312 | tf_op jit(solution)/shard_map/ppermute | solution.py:686
  115.2 2.5 %shard_map.147 = f32[896,4096]{1,0:T(8,128)} custom-call(bf16[64,896]{1,0:T(8,128)(2,1)S(1)} %get-tuple-element.232.left_ref, bf16[64,4096]{1,0:T(8,128)(2,1)S(1)} %get-tuple-element.220.right_ref, f32[896,4096]{1,0:T(8,128)} %shard_map.145.refs_0_), custom_call_target="tpu_custom_call", output_to_operand_aliasing={{}: (2, {})} | custom-call | flops 134217728 | bytes 4194304 | tf_op jit(solution)/shard_map/pallas_call | solution.py:488
  119.1 1.9 %shard_map.148 = bf16[128,4096]{1,0:T(8,128)(2,1)} custom-call(s32[2]{0:T(128)} %pad_add_fusion.here_ref.refs_0_, s32[1,1,2]{2,1,0:T(1,128)S(1)} %copy-done.3, s32[1,1,2]{2,1,0:T(1,128)S(1)} %copy-done.5, s32[1,1,2]{2,1,0:T(1,128)S(1)} %collective-permute-done.10.other_blocks_ref, s32[1,1,2]{2,1,0:T(1,128)S(1)} %collective-permute-done.11.other_dest_ref, ...), custom_call_target="tpu_custom_call" | custom-call | tf_op jit(solution)/shard_map/pallas_call | solution.py:628
  (93 shorter events, 29.8 us)
Async XLA Ops:
  0.6 1.5 %collective-permute-start.10 = (s32[1,1,2]{2,1,0:T(1,128)}, s32[1,1,2]{2,1,0:T(1,128)S(1)}, u32[]{:S(2)}, u32[]{:S(2)}) collective-permute-start(s32[1,1,2]{2,1,0:T(1,128)} %blocks_ref.3), channel_id=1, source_target_pairs={{0,16},{16,0},{1,17},{17,1},{2,18},{18,2},{3,19},{19,3},{4,20},{20... | collective-permute-start | bytes 32 | tf_op jit(solution)/shard_map/ppermute | solution.py:648
  1.1 1.3 %collective-permute-start.11 = (s32[1,1,2]{2,1,0:T(1,128)}, s32[1,1,2]{2,1,0:T(1,128)S(1)}, u32[]{:S(2)}, u32[]{:S(2)}) collective-permute-start(s32[1,1,2]{2,1,0:T(1,128)} %dest_ref.3), channel_id=1, source_target_pairs={{0,16},{16,0},{1,17},{17,1},{2,18},{18,2},{3,19},{19,3},{4,20},{20... | collective-permute-start | bytes 32 | tf_op jit(solution)/shard_map/ppermute | solution.py:649
  5.8 10.1 %collective-permute-start.12 = (bf16[8,4224]{1,0:T(8,128)(2,1)S(1)}, bf16[8,4224]{1,0:T(8,128)(2,1)S(1)}, u32[]{:S(2)}, u32[]{:S(2)}) collective-permute-start(bf16[8,4224]{1,0:T(8,128)(2,1)S(1)} %get-tuple-element.190), channel_id=1, source_target_pairs={{0,1},{1,2},{2,3},{3,4},{4,5},{5,6},{6,7},{7,8},{8,9},{9,10},{10,1... | collective-permute-start | bytes 202760 | tf_op jit(solution)/shard_map/ppermute | solution.py:47
  9.2 6.8 %collective-permute-start.13 = (bf16[8,4224]{1,0:T(8,128)(2,1)S(1)}, bf16[8,4224]{1,0:T(8,128)(2,1)S(1)}, u32[]{:S(2)}, u32[]{:S(2)}) collective-permute-start(bf16[8,4224]{1,0:T(8,128)(2,1)S(1)} %get-tuple-element.189), channel_id=1, source_target_pairs={{0,4},{1,5},{2,6},{3,7},{4,0},{5,1},{6,2},{7,3},{8,12},{9,13},{10,... | collective-permute-start | bytes 202760 | tf_op jit(solution)/shard_map/ppermute | solution.py:41
  10.7 6.5 %collective-permute-start.14 = (bf16[8,4224]{1,0:T(8,128)(2,1)S(1)}, bf16[8,4224]{1,0:T(8,128)(2,1)S(1)}, u32[]{:S(2)}, u32[]{:S(2)}) collective-permute-start(bf16[8,4224]{1,0:T(8,128)(2,1)S(1)} %get-tuple-element.190), channel_id=1, source_target_pairs={{0,5},{1,6},{2,7},{3,0},{4,1},{5,2},{6,3},{7,12},{8,13},{9,14},{10... | collective-permute-start | bytes 202760 | tf_op jit(solution)/shard_map/ppermute | solution.py:49
  17.3 8.9 %collective-permute-start.15 = (bf16[2,8,4224]{2,1,0:T(8,128)(2,1)S(1)}, bf16[2,8,4224]{2,1,0:T(8,128)(2,1)S(1)}, u32[]{:S(2)}, u32[]{:S(2)}) collective-permute-start(bf16[2,8,4224]{2,1,0:T(8,128)(2,1)S(1)} %pad_maximum_fusion.6), channel_id=1, source_target_pairs={{0,8},{1,9},{2,10},{3,11},{4,12},{5,13},{6,14},{7,15},{8,0},{9,1},... | collective-permute-start | bytes 405512 | tf_op jit(solution)/shard_map/ppermute | solution.py:41
  26.2 5.5 %collective-permute-start.16 = (bf16[4,8,2048]{2,1,0:T(8,128)(2,1)S(1)}, bf16[4,8,2048]{2,1,0:T(8,128)(2,1)S(1)}, u32[]{:S(2)}, u32[]{:S(2)}) collective-permute-start(bf16[4,8,2048]{2,1,0:T(8,128)(2,1)S(1)} %pad_maximum_fusion.7), channel_id=1, source_target_pairs={{0,2},{1,3},{2,0},{3,1},{4,6},{5,7},{6,4},{7,5},{8,10},{9,11},{10,... | collective-permute-start | bytes 393224 | tf_op jit(solution)/shard_map/ppermute | solution.py:41
  27.7 5.6 %collective-permute-start.18 = (bf16[4,8,2176]{2,1,0:T(8,128)(2,1)S(1)}, bf16[4,8,2176]{2,1,0:T(8,128)(2,1)S(1)}, u32[]{:S(2)}, u32[]{:S(2)}) collective-permute-start(bf16[4,8,2176]{2,1,0:T(8,128)(2,1)S(1)} %pad_maximum_fusion.4), channel_id=1, source_target_pairs={{0,1},{1,0},{2,3},{3,2},{4,5},{5,4},{6,7},{7,6},{8,9},{9,8},{10,11... | collective-permute-start | bytes 417800 | tf_op jit(solution)/shard_map/ppermute | solution.py:41
  31.7 6.8 %collective-permute-start.17 = (bf16[8,8,2048]{2,1,0:T(8,128)(2,1)S(1)}, bf16[8,8,2048]{2,1,0:T(8,128)(2,1)S(1)}, u32[]{:S(2)}, u32[]{:S(2)}) collective-permute-start(bf16[8,8,2048]{2,1,0:T(8,128)(2,1)S(1)} %pad_maximum_fusion.3), channel_id=1, source_target_pairs={{0,1},{1,0},{2,3},{3,2},{4,5},{5,4},{6,7},{7,6},{8,9},{9,8},{10,11... | collective-permute-start | bytes 786440 | tf_op jit(solution)/shard_map/ppermute | solution.py:41
  33.4 6.6 %collective-permute-start.19 = (bf16[8,8,2176]{2,1,0:T(8,128)(2,1)S(1)}, bf16[8,8,2176]{2,1,0:T(8,128)(2,1)S(1)}, u32[]{:S(2)}, u32[]{:S(2)}) collective-permute-start(bf16[8,8,2176]{2,1,0:T(8,128)(2,1)S(1)} %pad_maximum_fusion.2), channel_id=1, source_target_pairs={{0,2},{1,3},{2,0},{3,1},{4,6},{5,7},{6,4},{7,5},{8,10},{9,11},{10,... | collective-permute-start | bytes 835592 | tf_op jit(solution)/shard_map/ppermute | solution.py:41
  53.3 4.7 %collective-permute-start = (bf16[8,4224]{1,0:T(8,128)(2,1)S(1)}, bf16[8,4224]{1,0:T(8,128)(2,1)S(1)}, u32[]{:S(2)}, u32[]{:S(2)}) collective-permute-start(bf16[8,4224]{1,0:T(8,128)(2,1)S(1)} %get-tuple-element.86), channel_id=1, source_target_pairs={{0,4},{1,5},{2,6},{3,7},{4,0},{5,1},{6,2},{7,3},{8,12},{9,13},{10,... | collective-permute-start | bytes 202760 | tf_op jit(solution)/shard_map/cond/branch_1_fun/ppermute | solution.py:41
  58.0 6.6 %collective-permute-start.1 = (bf16[8,4224]{1,0:T(8,128)(2,1)S(1)}, bf16[8,4224]{1,0:T(8,128)(2,1)S(1)}, u32[]{:S(2)}, u32[]{:S(2)}) collective-permute-start(bf16[8,4224]{1,0:T(8,128)(2,1)S(1)} %fusion), channel_id=1, source_target_pairs={{0,8},{1,9},{2,10},{3,11},{4,12},{5,13},{6,14},{7,15},{8,0},{9,1},... | collective-permute-start | bytes 202760 | tf_op jit(solution)/shard_map/cond/branch_1_fun/ppermute | solution.py:41
  64.7 4.4 %collective-permute-start.2 = (bf16[8,4224]{1,0:T(8,128)(2,1)S(1)}, bf16[8,4224]{1,0:T(8,128)(2,1)S(1)}, u32[]{:S(2)}, u32[]{:S(2)}) collective-permute-start(bf16[8,4224]{1,0:T(8,128)(2,1)S(1)} %fusion.2), channel_id=1, source_target_pairs={{0,2},{1,3},{2,0},{3,1},{4,6},{5,7},{6,4},{7,5},{8,10},{9,11},{10,... | collective-permute-start | bytes 202760 | tf_op jit(solution)/shard_map/cond/branch_1_fun/ppermute | solution.py:41
  69.1 4.4 %collective-permute-start.3 = (bf16[8,4224]{1,0:T(8,128)(2,1)S(1)}, bf16[8,4224]{1,0:T(8,128)(2,1)S(1)}, u32[]{:S(2)}, u32[]{:S(2)}) collective-permute-start(bf16[8,4224]{1,0:T(8,128)(2,1)S(1)} %fusion.1), channel_id=1, source_target_pairs={{0,1},{1,0},{2,3},{3,2},{4,5},{5,4},{6,7},{7,6},{8,9},{9,8},{10,11... | collective-permute-start | bytes 202760 | tf_op jit(solution)/shard_map/cond/branch_1_fun/ppermute | solution.py:41
  73.7 1.3 %collective-permute-start.4 = (bf16[8,4096]{1,0:T(8,128)(2,1)S(1)}, bf16[8,4096]{1,0:T(8,128)(2,1)S(1)}, u32[]{:S(2)}, u32[]{:S(2)}) collective-permute-start(bf16[8,4096]{1,0:T(8,128)(2,1)S(1)} %branch_1_fun.8), channel_id=1, source_target_pairs={{0,16},{16,0},{1,17},{17,1},{2,18},{18,2},{3,19},{19,3},{4,20},{20... | collective-permute-start | bytes 196616 | tf_op jit(solution)/shard_map/cond/branch_1_fun/ppermute | solution.py:669
  83.3 9.7 %collective-permute-start.20 = (bf16[9,8,2176]{2,1,0:T(8,128)(2,1)}, bf16[9,8,2176]{2,1,0:T(8,128)(2,1)S(1)}, u32[]{:S(2)}, u32[]{:S(2)}) collective-permute-start(bf16[9,8,2176]{2,1,0:T(8,128)(2,1)} %get-tuple-element.250), channel_id=1, source_target_pairs={{0,1},{1,0},{2,3},{3,2},{4,5},{5,4},{6,7},{7,6},{8,9},{9,8},{10,11... | collective-permute-start | bytes 940040 | tf_op jit(solution)/shard_map/ppermute | solution.py:41
  93.2 5.7 %collective-permute-start.21 = (bf16[5,8,2176]{2,1,0:T(8,128)(2,1)S(1)}, bf16[5,8,2176]{2,1,0:T(8,128)(2,1)S(1)}, u32[]{:S(2)}, u32[]{:S(2)}) collective-permute-start(bf16[5,8,2176]{2,1,0:T(8,128)(2,1)S(1)} %maximum_maximum_fusion), channel_id=1, source_target_pairs={{0,2},{1,3},{2,0},{3,1},{4,6},{5,7},{6,4},{7,5},{8,10},{9,11},{10,... | collective-permute-start | bytes 522248 | tf_op jit(solution)/shard_map/ppermute | solution.py:41
  99.0 7.2 %collective-permute-start.22 = (bf16[3,8,2176]{2,1,0:T(8,128)(2,1)S(1)}, bf16[3,8,2176]{2,1,0:T(8,128)(2,1)S(1)}, u32[]{:S(2)}, u32[]{:S(2)}) collective-permute-start(bf16[3,8,2176]{2,1,0:T(8,128)(2,1)S(1)} %maximum_maximum_fusion.1), channel_id=1, source_target_pairs={{0,8},{1,9},{2,10},{3,11},{4,12},{5,13},{6,14},{7,15},{8,0},{9,1},... | collective-permute-start | bytes 313352 | tf_op jit(solution)/shard_map/ppermute | solution.py:41
  106.4 5.6 %collective-permute-start.23 = (bf16[2,8,2176]{2,1,0:T(8,128)(2,1)S(1)}, bf16[2,8,2176]{2,1,0:T(8,128)(2,1)S(1)}, u32[]{:S(2)}, u32[]{:S(2)}) collective-permute-start(bf16[2,8,2176]{2,1,0:T(8,128)(2,1)S(1)} %maximum_maximum_fusion.2), channel_id=1, source_target_pairs={{0,4},{1,5},{2,6},{3,7},{4,0},{5,1},{6,2},{7,3},{8,12},{9,13},{10,... | collective-permute-start | bytes 208904 | tf_op jit(solution)/shard_map/ppermute | solution.py:41
  112.8 6.4 %copy-start.3 = (s32[1,1,2]{2,1,0:T(1,128)S(1)}, s32[1,1,2]{2,1,0:T(1,128)}, u32[]{:S(2)}) copy-start(s32[1,1,2]{2,1,0:T(1,128)} %blocks_ref.3) | copy-start | bytes 28
  112.8 6.4 %copy-start.5 = (s32[1,1,2]{2,1,0:T(1,128)S(1)}, s32[1,1,2]{2,1,0:T(1,128)}, u32[]{:S(2)}) copy-start(s32[1,1,2]{2,1,0:T(1,128)} %dest_ref.3) | copy-start | bytes 28
  112.8 4.9 %collective-permute-start.24 = (bf16[8,2048]{1,0:T(8,128)(2,1)S(1)}, bf16[8,2048]{1,0:T(8,128)(2,1)S(1)}, u32[]{:S(2)}, u32[]{:S(2)}) collective-permute-start(bf16[8,2048]{1,0:T(8,128)(2,1)S(1)} %get-tuple-element.231.own_ref), channel_id=1, source_target_pairs={{0,15},{1,0},{2,1},{3,2},{4,3},{5,4},{6,5},{7,6},{8,7},{9,8},{10,9... | collective-permute-start | bytes 98312 | tf_op jit(solution)/shard_map/ppermute | solution.py:686
  115.2 3.1 %collective-permute-start.25 = (bf16[8,2048]{1,0:T(8,128)(2,1)S(1)}, bf16[8,2048]{1,0:T(8,128)(2,1)S(1)}, u32[]{:S(2)}, u32[]{:S(2)}) collective-permute-start(bf16[8,2048]{1,0:T(8,128)(2,1)S(1)} %get-tuple-element.231.own_ref), channel_id=1, source_target_pairs={{0,16},{16,0},{1,17},{17,1},{2,18},{18,2},{3,19},{19,3},{4,20},{20... | collective-permute-start | bytes 98312 | tf_op jit(solution)/shard_map/ppermute | solution.py:687
  117.7 1.4 %collective-permute-start.26 = (bf16[8,2048]{1,0:T(8,128)(2,1)S(1)}, bf16[8,2048]{1,0:T(8,128)(2,1)S(1)}, u32[]{:S(2)}, u32[]{:S(2)}) collective-permute-start(bf16[8,2048]{1,0:T(8,128)(2,1)S(1)} %collective-permute-done.24.back_ref), channel_id=1, source_target_pairs={{0,16},{16,0},{1,17},{17,1},{2,18},{18,2},{3,19},{19,3},{4,20},{20... | collective-permute-start | bytes 98312 | tf_op jit(solution)/shard_map/ppermute | solution.py:689
  (7 other events, 14.1 us)
where the time goes:
time: 121 us
  Pallas kernels  66.6 us (55%)
  starting transfers between devices  29 us (24%)
  waiting for transfers between devices  18.5 us (15%)
  between operations  2.96 us (2%)
  local copies, waits for them, and re-layouts  2.57 us (2%)
  other arithmetic  1.44 us (1%)
    pallas_call x6, Pallas kernels, weight_grad(): pl.pallas_call(functools.partial(outer_kernel, tile, first, count), out_s...  21.8 us
    ppermute x14, starting transfers between devices, exchange(): return lax.ppermute(block, 'ctx', [(i, i ^ mask) for i in range(peers)])  21.2 us
    pallas_call x2, Pallas kernels, layer_pass(): pl.pallas_call(functools.partial(layer_kernel, again is not None, stream,...  20.7 us
    pallas_call x6, Pallas kernels, fetch(): pl.pallas_call(fetch_kernel, out_shape=pltpu.VMEM(weight.shape, weight.dt...  19 us
    ppermute x14, waiting for transfers between devices, exchange(): return lax.ppermute(block, 'ctx', [(i, i ^ mask) for i in range(peers)])  15.8 us
    ppermute x1, starting transfers between devices, first_pair(): lax.ppermute(handed, 'ctx', [(i, (i + 1) % peers) for i in range(peers)])  2.75 us
    ppermute x1, starting transfers between devices, on_device(): lax.ppermute(delta, 'ctx', [(i, (i - 1) % peers) for i in range(peers)])  2.42 us
  transfers between devices with their start and end apart: 22, of which 12 were waited for; matrix products, arithmetic and copies ran while one was open for 2% of the time, Pallas kernels for 34%

commit v1 on v0

--- a/solution.py
+++ b/solution.py
@@ -12,11 +12,12 @@
 LANES = 128
 CHUNK = 512
 WIDE = 1024
-SHARES = (7, 4, 4, 4, 2, 0)
+PLAN_TILES = 14
+PLAN = (((0, 0, 14),), ((1, 0, 8),), ((2, 0, 11),), ((1, 8, 6), (2, 11, 3)))
 GROUP = 16
 TILE = 256
 VMEM_LIMIT = 10 * 1024 * 1024
-STREAM_LIMIT = 52 * 1024 * 1024
+STREAM_LIMIT = 32 * 1024 * 1024
 SMALL_LIMIT = 6 * 1024 * 1024
 
 F32 = jnp.float32
@@ -41,6 +42,17 @@
     return lax.ppermute(block, "ctx", [(i, i ^ mask) for i in range(peers)])
 
 
+def choose_kernel(kept_ref, came_ref, far_kept_ref, far_came_ref, pair_ref):
+    used = kept_ref.shape[1] - LANES + 3
+
+    def choose(kept, came):
+        keeps = kept[:, used : used + 1].astype(F32) > 0.5
+        return jnp.where(keeps, kept[...].astype(F32), came[...].astype(F32)).astype(BF16)
+
+    pair_ref[0] = choose(kept_ref, came_ref)
+    pair_ref[1] = choose(far_kept_ref, far_came_ref)
+
+
 def first_pair(kept, handed, weight):
     peers = lax.axis_size("ctx")
     mask = hop_order(peers)[0]
@@ -48,10 +60,14 @@
     far_kept = exchange(kept, mask)
     far_came = lax.ppermute(handed, "ctx", [(i, ((i + 1) % peers) ^ mask) for i in range(peers)])
     came, weight = beside(came, handed, weight)
-    used = kept.shape[1] - LANES + 3
-    mine = jnp.where(kept[:1, used : used + 1] > 0.5, kept, came)
-    far = jnp.where(far_kept[:1, used : used + 1] > 0.5, far_kept, far_came)
-    return mine, jnp.stack([mine, far]), weight
+    pair = pl.pallas_call(
+        choose_kernel,
+        out_shape=jax.ShapeDtypeStruct((2,) + kept.shape, BF16),
+        in_specs=[VMEM_SPEC] * 4,
+        out_specs=VMEM_SPEC,
+        compiler_params=pltpu.CompilerParams(vmem_limit_bytes=SMALL_LIMIT),
+    )(kept, came, far_kept, far_came)
+    return pair, weight
 
 
 def gather_all(held, weights):
@@ -80,24 +96,29 @@
     return (first, second), (up_w, down_w)
 
 
-def scatter_sum(chunks, sent, stats, outers):
-    rows = stats.shape[0]
-    masks = hop_order(lax.axis_size("ctx"))[::-1]
+def scatter_sum(keep, sent, outers):
+    peers = lax.axis_size("ctx")
+    half = keep.shape[0] - 2
+    chunks, stats = keep[:half], keep[half, :BLOCK]
+    masks = hop_order(peers)[::-1]
     for step, mask in enumerate(masks):
         if step > 0:
             half = chunks.shape[0] // 2
             high = lax.reduce_precision(stats, 8, 7)
             both = jnp.concatenate([high, stats - high], axis=0).astype(BF16)
             sent = jnp.concatenate([chunks[half:].astype(BF16), both[None]], axis=0)
-            chunks = chunks[:half]
-        received = outers.beside(exchange(sent, mask), sent)
-        if mask == masks[-1]:
-            break
-        received = received.astype(F32)
-        half = chunks.shape[0]
-        chunks = chunks + received[:half]
-        stats = stats + received[half, :rows] + received[half, rows:]
-    return chunks[0], stats, received
+        received = exchange(sent, mask)
+        if mask != masks[-1]:
+            received = outers.beside(received, sent)
+            chunks = chunks[:half] + received[:half].astype(F32)
+            stats = stats + received[half, :BLOCK].astype(F32)
+            stats = stats + received[half, BLOCK:].astype(F32)
+    near = lax.ppermute(
+        chunks[0].astype(BF16), "ctx", [(i, (i - 1) % peers) for i in range(peers)]
+    )
+    far = lax.ppermute(sent[0], "ctx", [(i, ((i ^ masks[-1]) - 1) % peers) for i in range(peers)])
+    received = outers.beside(received, sent)
+    return chunks[0], stats, received, near, far
 
 
 def sum_all(rows, weights):
@@ -127,11 +148,11 @@
 
 
 def pick_kernel(
-    here_ref, blocks_ref, dest_ref, other_blocks_ref, other_dest_ref, saved_ref, grad_ref,
+    blocks_ref, dest_ref, other_blocks_ref, other_dest_ref, saved_ref, grad_ref,
     keep_ref, hand_ref, groups, sems,
 ):
     model_dim = saved_ref.shape[1]
-    me = here_ref[1]
+    me = lax.axis_index("ctx")
     slots = route_slots(blocks_ref, dest_ref, me)
     copies = []
     for slot, (block, _) in enumerate(slots):
@@ -170,38 +191,42 @@
         out[:, model_dim:] = meta.astype(BF16)
 
 
-def pick_blocks(here, routes, saved, grad):
+def pick_blocks(routes, saved, grad):
     model_dim = saved.shape[1]
     shape = jax.ShapeDtypeStruct((8, model_dim + LANES), BF16)
     return pl.pallas_call(
         pick_kernel,
         out_shape=(shape, shape),
-        in_specs=[SMEM_SPEC] * 5 + [ANY_SPEC, ANY_SPEC],
+        in_specs=[SMEM_SPEC] * 4 + [ANY_SPEC, ANY_SPEC],
         out_specs=(VMEM_SPEC, VMEM_SPEC),
         scratch_shapes=[
             pltpu.VMEM((2, 2, GROUP, model_dim), BF16),
             pltpu.SemaphoreType.DMA((2, 2)),
         ],
         compiler_params=pltpu.CompilerParams(vmem_limit_bytes=SMALL_LIMIT),
-    )(here, *routes, *(pltpu.with_memory_space_constraint(a, pltpu.HBM) for a in (saved, grad)))
+    )(
+        *(pltpu.with_memory_space_constraint(a, pltpu.HBM) for a in routes[:2]),
+        *routes[2:],
+        *(pltpu.with_memory_space_constraint(a, pltpu.HBM) for a in (saved, grad)),
+    )
 
 
 def layer_kernel(with_delta, stream, tile, *refs):
     if with_delta:
         delta_ref, active_ref, up_slope_ref, hidden_ref = refs[:4]
         refs = refs[4:]
-    here_ref, first_ref, second_ref, gain_ref, router_ref, gate_w, up_w, down_w = refs[:8]
-    refs = refs[8:]
-    gate_grad_ref, up_grad_ref, scaled_ref, keep_ref, sent_ref, stat_ref = refs[:6]
-    refs = refs[6:]
+    first_ref, second_ref, gain_ref, router_ref, gate_w, up_w, down_w = refs[:7]
+    refs = refs[7:]
+    gate_grad_ref, up_grad_ref, scaled_ref, keep_ref, sent_ref = refs[:5]
+    refs = refs[5:]
     if not with_delta:
         hidden_ref, normed_ref, active_ref, up_slope_ref = refs[:4]
         shared_part_ref, shared_x_ref, case_ref = refs[4:7]
         refs = refs[7:]
-    picked_s, up_s = refs[:2]
+    picked_s, up_s, gate_rows, up_rows = refs[:4]
     waits = ()
     if stream:
-        *held, sems = refs[2:]
+        *held, sems = refs[4:]
         copies = [
             pltpu.make_async_copy(source, target, sems.at[index])
             for index, (source, target) in enumerate(zip((down_w, gate_w, up_w), held))
@@ -214,7 +239,7 @@
     quarter = half_pairs // 2
     rows = half_pairs * 8
     model_dim = scaled_ref.shape[1]
-    ff_local = gate_grad_ref.shape[1]
+    ff_local = gate_grad_ref.shape[0]
     middle = model_dim // 2
 
     def split(ref, start, width):
@@ -255,7 +280,7 @@
     place = rank.astype(jnp.int32) * BLOCK + row_b % BLOCK
     chosen = jnp.where((place == row_a) & (across[2:3] > 0.5), 1.0, 0.0).astype(BF16)
     if with_delta:
-        lower = jnp.where(here_ref[0] == 0, 1.0, 0.0).astype(BF16)
+        lower = jnp.where(lax.axis_index("pipe") == 0, 1.0, 0.0).astype(BF16)
         spread = chosen[: delta_ref.shape[0]] * lower
     else:
         blocks = jnp.sum(across[2:3]) * (1.0 / BLOCK)
@@ -296,21 +321,25 @@
             activated = gate * sigma
             up_slope = up * (sigma * (1.0 + gate * (1.0 - sigma)))
             hidden = (activated * up).astype(BF16)
-            hidden_ref[:, at] = hidden.T
+            hidden_ref[at, :] = hidden
             active_ref[at, :] = activated
             up_slope_ref[at, :] = up_slope
-        gate_grad_ref[:, at] = (hidden_grad * up_slope).astype(BF16).T
-        up_grad_ref[:, at] = (hidden_grad * activated).astype(BF16).T
+        gate_grad = (hidden_grad * up_slope).astype(BF16)
+        up_grad = (hidden_grad * activated).astype(BF16)
+        gate_grad_ref[at, :] = gate_grad
+        up_grad_ref[at, :] = up_grad
+        gate_rows[:, at] = gate_grad.T
+        up_rows[:, at] = up_grad.T
         if with_delta:
-            hidden = hidden_ref[:, at].T
+            hidden = hidden_ref[at, :]
         row_sums = row_sums + jnp.sum(hidden_grad * hidden.astype(F32), axis=0, keepdims=True).T
     logit_part = row_sums * (1.0 - router)
 
     low = lax.broadcasted_iota(jnp.int32, (half_pairs, 8, 1), 1) < BLOCK
 
     def store(even, odd, at):
-        keep_ref[:, 0, :, at] = even[:quarter]
-        keep_ref[:, 1, :, at] = odd[:quarter]
+        keep_ref[:quarter, 0, :, at] = even[:quarter]
+        keep_ref[:quarter, 1, :, at] = odd[:quarter]
         for q in range(quarter):
             sent_ref[2 * q, :, at] = even[quarter + q].astype(BF16)
             sent_ref[2 * q + 1, :, at] = odd[quarter + q].astype(BF16)
@@ -326,8 +355,8 @@
         for second in range(2):
             cols = pl.ds(pl.multiple_of(c * WIDE + second * middle, WIDE), WIDE)
             grad = jnp.dot(
-                gate_grad_ref[...], gate_w[:, cols], preferred_element_type=F32
-            ) + jnp.dot(up_grad_ref[...], up_w[:, cols], preferred_element_type=F32)
+                gate_rows[...], gate_w[:, cols], preferred_element_type=F32
+            ) + jnp.dot(up_rows[...], up_w[:, cols], preferred_element_type=F32)
             x = picked_s[:, cols].astype(F32)
             gains.append(jnp.sum(grad * (x * inverse), axis=0, keepdims=True))
             routers.append(jnp.sum(logit_part * x, axis=0, keepdims=True))
@@ -344,7 +373,7 @@
         )
         stats = jnp.concatenate(gains + routers, axis=0)
         high = stats.astype(BF16).astype(F32)
-        stat_ref[:, at] = stats
+        keep_ref[quarter, 0, :BLOCK, at] = stats
         sent_ref[2 * quarter, :, at] = jnp.concatenate([high, stats - high], axis=0).astype(BF16)
         return carry
 
@@ -356,7 +385,7 @@
         ).astype(BF16)
     wide = wide.reshape(half_pairs, 8, LANES)
     store(wide, pltpu.roll(wide, BLOCK, 1), pl.ds(middle, LANES))
-    stat_ref[:, middle:] = jnp.zeros((4, LANES), F32)
+    keep_ref[quarter, 0, :BLOCK, middle:] = jnp.zeros((BLOCK, LANES), F32)
     sent_ref[2 * quarter, :, middle:] = jnp.zeros((8, LANES), BF16)
 
 
@@ -394,7 +423,7 @@
     return received, fetched
 
 
-def layer_pass(here, pay, gain, router, weights, few, again=None, stream=False):
+def layer_pass(pay, gain, router, weights, few, again=None, stream=False):
     peers = pay[0].shape[0]
     rows = peers * BLOCK
     ff_local, model_dim = weights[0].shape
@@ -402,22 +431,21 @@
     pairs = [part.reshape((peers // 2, 2) + part.shape[1:]) for part in pay]
     if not stream:
         weights = [pltpu.with_memory_space_constraint(w, pltpu.VMEM) for w in weights]
-    operands = [here, *pairs, gain, router, *weights]
-    in_specs = [SMEM_SPEC] + [VMEM_SPEC] * 4 + [ANY_SPEC if stream else VMEM_SPEC] * 3
-    scratch = [pltpu.VMEM((rows, model_dim), BF16)] * 2
+    operands = [*pairs, gain, router, *weights]
+    in_specs = [VMEM_SPEC] * 4 + [ANY_SPEC if stream else VMEM_SPEC] * 3
+    scratch = [pltpu.VMEM((rows, model_dim), BF16)] * 2 + [pltpu.VMEM((rows, ff_local), BF16)] * 2
     if stream:
         scratch += [pltpu.VMEM((ff_local, model_dim), BF16)] * 3
         scratch += [pltpu.SemaphoreType.DMA((3,))]
-    small = jax.ShapeDtypeStruct((rows, ff_local), BF16)
+    small = jax.ShapeDtypeStruct((ff_local, rows), BF16)
     large = jax.ShapeDtypeStruct((rows, model_dim), BF16)
     tall = jax.ShapeDtypeStruct((ff_local, rows), F32)
     out_shape = [
         small,
         small,
         large,
-        jax.ShapeDtypeStruct((peers // 4, 2, 8, wide), F32),
+        jax.ShapeDtypeStruct((peers // 4 + 1, 2, 8, wide), F32),
         jax.ShapeDtypeStruct((peers // 2 + 1, 8, wide), BF16),
-        jax.ShapeDtypeStruct((4, wide), F32),
     ]
     out_specs = [VMEM_SPEC] * len(out_shape)
     if again is None:
@@ -449,56 +477,67 @@
             transcendentals=rows * ff_local,
         ),
     )(*operands)
-    return tuple(outs[:6]), tuple(outs[6:])
-
-
-def outer_kernel(tile, first, count, left_ref, right_ref, *refs):
-    out_ref, ring, sems = refs[-3:]
+    return tuple(outs[:5]), tuple(outs[5:])
+
+
+def outer_kernel(tile, pieces, operands, *refs):
+    outs = refs[operands : operands + len(pieces)]
+    ring, sems = refs[-2:]
     depth = ring.shape[0]
     copies = []
-    for t in range(count):
-        slot = t % depth
-        if t >= depth:
-            copies[t - depth].wait()
-        ring[slot] = lax.dot_general(
-            left_ref[:, (first + t) * tile : (first + t + 1) * tile],
-            right_ref[...],
-            (((0,), (0,)), ((), ())),
-            preferred_element_type=F32,
-        )
-        copy = pltpu.make_async_copy(
-            ring.at[slot], out_ref.at[pl.ds((first + t) * tile, tile)], sems.at[slot]
-        )
-        copy.start()
-        copies.append(copy)
+    for (first, count, left, right), out_ref in zip(pieces, outs):
+        for t in range(first, first + count):
+            slot = len(copies) % depth
+            if len(copies) >= depth:
+                copies[len(copies) - depth].wait()
+            at = pl.ds(t * tile, tile)
+            ring[slot] = jnp.dot(refs[left][at, :], refs[right][...], preferred_element_type=F32)
+            copy = pltpu.make_async_copy(ring.at[slot], out_ref.at[at], sems.at[slot])
+            copy.start()
+            copies.append(copy)
     for copy in copies[-depth:]:
         copy.wait()
 
 
 def outer_tile(ff_local):
-    return LANES if ff_local % LANES == 0 else ff_local
-
-
-def weight_grad(left, right, first, count, into):
-    rows, ff_local = left.shape
-    model_dim = right.shape[1]
+    return 64 if ff_local % 64 == 0 else 32
+
+
+def weight_grads(pieces, factors, results):
+    ff_local, rows = factors[0][0].shape
+    model_dim = factors[0][1].shape[1]
     tile = outer_tile(ff_local)
-    depth = min(4, count)
-    operands = [left, right] + ([] if into is None else [into])
+    total = sum(count for _, _, count in pieces)
+    depth = min(8, total)
+    operands, specs, plan, aliases = [], [], [], {}
+
+    def operand(value, spec):
+        for index, known in enumerate(operands):
+            if known is value:
+                return index
+        operands.append(value)
+        specs.append(spec)
+        return len(operands) - 1
+
+    for index, (which, first, count) in enumerate(pieces):
+        left, right = (operand(value, VMEM_SPEC) for value in factors[which])
+        plan.append((first, count, left, right))
+        if results[which] is not None:
+            aliases[operand(results[which], ANY_SPEC)] = index
     return pl.pallas_call(
-        functools.partial(outer_kernel, tile, first, count),
-        out_shape=jax.ShapeDtypeStruct((ff_local, model_dim), F32),
-        in_specs=[VMEM_SPEC, VMEM_SPEC, ANY_SPEC][: len(operands)],
-        out_specs=ANY_SPEC,
-        input_output_aliases={} if into is None else {2: 0},
+        functools.partial(outer_kernel, tile, tuple(plan), len(operands)),
+        out_shape=(jax.ShapeDtypeStruct((ff_local, model_dim), F32),) * len(pieces),
+        in_specs=specs,
+        out_specs=(ANY_SPEC,) * len(pieces),
+        input_output_aliases=aliases,
         scratch_shapes=[
             pltpu.VMEM((depth, tile, model_dim), F32),
             pltpu.SemaphoreType.DMA((depth,)),
         ],
         compiler_params=pltpu.CompilerParams(vmem_limit_bytes=16 * 1024 * 1024),
         cost_estimate=pl.CostEstimate(
-            flops=2 * rows * count * tile * model_dim,
-            bytes_accessed=4 * count * tile * model_dim,
+            flops=2 * rows * total * tile * model_dim,
+            bytes_accessed=4 * total * tile * model_dim,
             transcendentals=0,
         ),
     )(*operands)
@@ -506,12 +545,14 @@
 
 class Outers:
     def __init__(self, factors, windows):
-        tiles = factors[0][0].shape[1] // outer_tile(factors[0][0].shape[1])
+        tiles = factors[0][0].shape[0] // outer_tile(factors[0][0].shape[0])
         self.factors = factors
         self.results = [None] * len(factors)
         total = tiles * len(factors)
-        shares = SHARES if windows == len(SHARES) else (1,) * windows
-        ends = [total * sum(shares[: i + 1]) // sum(shares) for i in range(windows)]
+        if windows == len(PLAN) and tiles == PLAN_TILES:
+            self.pieces = [list(piece) for piece in PLAN]
+            return
+        ends = [total * (i + 1) // windows for i in range(windows)]
         self.pieces = []
         for begin, end in zip([0] + ends[:-1], ends):
             piece = []
@@ -523,11 +564,18 @@
             self.pieces.append(piece)
 
     def beside(self, received, sent):
-        for which, first, count in self.pieces.pop(0):
-            left, right = self.factors[which]
-            left, _ = lax.optimization_barrier((left, sent))
-            result = weight_grad(left, right, first, count, self.results[which])
-            received, self.results[which] = lax.optimization_barrier((received, result))
+        pieces = self.pieces.pop(0)
+        if not pieces:
+            return received
+        factors = list(self.factors)
+        which = pieces[0][0]
+        left, right = factors[which]
+        left, _ = lax.optimization_barrier((left, sent))
+        factors[which] = (left, right)
+        written = weight_grads(pieces, factors, self.results)
+        received, *written = lax.optimization_barrier((received, *written))
+        for (which, _, _), result in zip(pieces, written):
+            self.results[which] = result
         return received
 
 
@@ -541,32 +589,37 @@
 
 
 def delta_kernel(
-    pay_ref, sum_ref, stat_ref, last_ref, gain_ref, router_ref, out_ref, gain_out_ref, router_out_ref
+    kept_ref, handed_ref, sum_ref, stat_ref, last_ref, near_ref, far_ref, gain_ref, router_ref,
+    out_ref, gain_out_ref, router_out_ref,
 ):
-    middle = out_ref.shape[1]
-    x = pay_ref[...].astype(F32)[:BLOCK, : 2 * middle]
-    sums = sum_ref[...] + last_ref[0].astype(F32)
-    far = last_ref[1].astype(F32)
-    stats = stat_ref[...] + far[:BLOCK] + far[BLOCK:]
-    grad = jnp.concatenate([sums[:BLOCK, :middle], sums[BLOCK:, :middle]], axis=1)
-    row_sum = sums[:BLOCK, middle : middle + 1]
-    delta = norm_backward(x, grad, row_sum, gain_ref[...], router_ref[...].astype(F32))
-    out_ref[...] = jnp.concatenate([delta[:, :middle], delta[:, middle:]], axis=0).astype(BF16)
+    middle = out_ref.shape[2]
+    kept_sum = sum_ref[...] + last_ref[0].astype(F32)
+    handed_sum = near_ref[...].astype(F32) + far_ref[...].astype(F32)
+    for slot, (pay, sums) in enumerate(((kept_ref, kept_sum), (handed_ref, handed_sum))):
+        x = pay[...].astype(F32)[:BLOCK, : 2 * middle]
+        grad = jnp.concatenate([sums[:BLOCK, :middle], sums[BLOCK:, :middle]], axis=1)
+        row_sum = sums[:BLOCK, middle : middle + 1]
+        delta = norm_backward(x, grad, row_sum, gain_ref[...], router_ref[...].astype(F32))
+        out_ref[slot] = jnp.concatenate([delta[:, :middle], delta[:, middle:]], axis=0).astype(
+            BF16
+        )
+    more = last_ref[1].astype(F32)
+    stats = stat_ref[...] + more[:BLOCK] + more[BLOCK:]
     for second in range(2):
         cols = slice(second * middle, (second + 1) * middle)
         gain_out_ref[:, cols] = stats[second : second + 1, :middle]
         router_out_ref[:, cols] = stats[2 + second : 3 + second, :middle]
 
 
-def delta_rows(pay, sums, stats, last, gain, router):
+def delta_rows(kept, handed, sums, gain, router):
     row = jax.ShapeDtypeStruct(gain.shape, F32)
     return pl.pallas_call(
         delta_kernel,
-        out_shape=(jax.ShapeDtypeStruct((8, sums.shape[1] - LANES), BF16), row, row),
-        in_specs=[VMEM_SPEC] * 6,
+        out_shape=(jax.ShapeDtypeStruct((2, 8, sums[0].shape[1] - LANES), BF16), row, row),
+        in_specs=[VMEM_SPEC] * 9,
         out_specs=(VMEM_SPEC,) * 3,
         compiler_params=pltpu.CompilerParams(vmem_limit_bytes=SMALL_LIMIT),
-    )(pay, sums, stats, last, gain, router)
+    )(kept, handed, *sums, gain, router)
 
 
 def shared_kernel(x_ref, sum_ref, gain_ref, router_ref, out_ref):
@@ -594,13 +647,14 @@
 
 
 def add_kernel(
-    here_ref, blocks_ref, dest_ref, other_blocks_ref, other_dest_ref,
-    own_ref, back_ref, other_ref, other_back_ref, grad_ref, out_ref,
+    blocks_ref, dest_ref, other_blocks_ref, other_dest_ref,
+    own_ref, other_ref, grad_ref, out_ref,
 ):
-    middle = own_ref.shape[1]
-    lower = here_ref[0] == 0
-    mine = route_slots(blocks_ref, dest_ref, here_ref[1])
-    theirs = route_slots(other_blocks_ref, other_dest_ref, here_ref[1])
+    middle = own_ref.shape[2]
+    lower = lax.axis_index("pipe") == 0
+    me = lax.axis_index("ctx")
+    mine = route_slots(blocks_ref, dest_ref, me)
+    theirs = route_slots(other_blocks_ref, other_dest_ref, me)
     out_ref[...] = grad_ref[...]
     row = lax.broadcasted_iota(jnp.int32, (GROUP, 1), 0)
 
@@ -615,29 +669,27 @@
                 out_ref[at, cols].astype(F32) + jnp.where(mask, spread, 0.0)
             ).astype(BF16)
 
-    for slot, (own, other) in enumerate(((own_ref, other_ref), (back_ref, other_back_ref))):
+    for slot in range(2):
         block = jnp.where(lower, theirs[slot][0], mine[slot][0])
         used = jnp.where(lower, theirs[slot][1], mine[slot][1])
-        deltas = jnp.where(lower, other[...].astype(F32), own[...].astype(F32))
-        add(block, used, deltas)
-    for slot, own in enumerate((own_ref, back_ref)):
-        add(mine[slot][0], mine[slot][1] & lower, own[...].astype(F32))
-
-
-def add_rows(here, routes, deltas, grad):
+        add(block, used, jnp.where(lower, other_ref[slot].astype(F32), own_ref[slot].astype(F32)))
+    for slot in range(2):
+        add(mine[slot][0], mine[slot][1] & lower, own_ref[slot].astype(F32))
+
+
+def add_rows(routes, own, other, grad):
     return pl.pallas_call(
         add_kernel,
         out_shape=jax.ShapeDtypeStruct(grad.shape, BF16),
-        in_specs=[SMEM_SPEC] * 5 + [VMEM_SPEC] * 5,
+        in_specs=[SMEM_SPEC] * 4 + [VMEM_SPEC] * 3,
         out_specs=VMEM_SPEC,
         compiler_params=pltpu.CompilerParams(vmem_limit_bytes=SMALL_LIMIT),
-    )(here, *routes, *deltas, grad)
+    )(*routes, own, other, grad)
 
 
 def on_device(saved, grad_out, route_blocks, route_dest, gain, w_router, w_gate, w_up, w_down):
     sections = lax.axis_size("pipe")
     peers = lax.axis_size("ctx")
-    here = jnp.stack([lax.axis_index("pipe"), lax.axis_index("ctx")]).astype(jnp.int32)
     tokens = saved[0]
     model_dim = tokens.shape[1]
 
@@ -648,11 +700,11 @@
         lax.ppermute(route_blocks, "pipe", swap),
         lax.ppermute(route_dest, "pipe", swap),
     )
-    kept_rows, handed_rows = pick_blocks(here, routes, tokens, grad_out)
-    pay_mine, pair, gate_w = first_pair(kept_rows, handed_rows, w_gate[0])
+    kept_rows, handed_rows = pick_blocks(routes, tokens, grad_out)
+    pair, gate_w = first_pair(kept_rows, handed_rows, w_gate[0])
     pay, (up_w, down_w) = gather_all(pair, (w_up[0], w_down[0]))
     few = 2 * BLOCK
-    run = functools.partial(layer_pass, here, pay, gain, w_router)
+    run = functools.partial(layer_pass, pay, gain, w_router)
     state, saved_parts = run((gate_w, up_w, down_w), few)
     hidden, normed, active, up_slope, shared_part, shared_x, case = saved_parts
 
@@ -675,19 +727,13 @@
     state = lax.switch(
         case[0], (lambda state: state, corrected(few), corrected(peers * BLOCK)), state
     )
-    gate_grad, up_grad, scaled, keep, sent, stats = state
-
-    outers = Outers(
-        ((hidden, scaled), (gate_grad, normed), (up_grad, normed)), len(hop_order(peers)) + 2
-    )
-    keep = keep.reshape((peers // 2,) + keep.shape[2:])
-    sums, stats, last = scatter_sum(keep, sent, stats, outers)
-    delta, grad_gain, grad_router = delta_rows(pay_mine, sums, stats, last, gain, w_router)
-    back = lax.ppermute(delta, "ctx", [(i, (i - 1) % peers) for i in range(peers)])
+    gate_grad, up_grad, scaled, keep, sent = state
+
+    outers = Outers(((hidden, scaled), (gate_grad, normed), (up_grad, normed)), len(hop_order(peers)))
+    sums = scatter_sum(keep.reshape((-1,) + keep.shape[2:]), sent, outers)
+    delta, grad_gain, grad_router = delta_rows(kept_rows, handed_rows, sums, gain, w_router)
     other = lax.ppermute(delta, "pipe", swap)
-    back = outers.beside(back, delta)
-    other_back = outers.beside(lax.ppermute(back, "pipe", swap), back)
-    grad_inputs = add_rows(here, routes, (delta, back, other, other_back), grad_out)
+    grad_inputs = add_rows(routes, delta, other, grad_out)
     grad_down, grad_gate, grad_up = outers.results
     return (
         grad_inputs[None],

time: 121 us -> 82.8 us (0.68)
  Pallas kernels: 66.6 us -> 43 us
  starting transfers between devices: 29 us -> 23.2 us
  waiting for transfers between devices: 18.5 us -> 13.8 us
  local copies, waits for them, and re-layouts: 2.57 us -> 0.13 us
  between operations: 2.96 us -> 1.58 us
    pallas_call x2 -> x1, Pallas kernels: 20.7 us -> 10.9 us  [layer_pass(): pl.pallas_call(functools.partial(layer_kernel, again is not None, stream,...]
    pallas_call x6 -> x3, Pallas kernels: 19 us -> 9.49 us  [fetch(): pl.pallas_call(fetch_kernel, out_shape=pltpu.VMEM(weight.shape, weight.dt...]
    ppermute x14 -> x10, starting transfers between devices: 21.2 us -> 13.2 us  [exchange(): return lax.ppermute(block, 'ctx', [(i, i ^ mask) for i in range(peers)])]
    ppermute x14 -> x10, waiting for transfers between devices: 15.8 us -> 9.76 us  [exchange(): return lax.ppermute(block, 'ctx', [(i, i ^ mask) for i in range(peers)])]
    pallas_call x8 -> x6, Pallas kernels: 22.9 us -> 18.7 us  [the longest x4 17.8 us: weight_grads(): pl.pallas_call(functools.partial(outer_kernel, tile, tuple(plan), len(ope...]
    ppermute x3 -> x2, starting transfers between devices: 3.07 us -> 5.32 us  [the longest x1 2.93 us: scatter_sum(): lax.ppermute(sent[0], 'ctx', [(i, ((i ^ masks[-1]) - 1) % peers) for i in...]
    ppermute x3 -> x2, waiting for transfers between devices: 2.1 us -> 0.01 us  [the longest x1 0.01 us: scatter_sum(): lax.ppermute(sent[0], 'ctx', [(i, ((i ^ masks[-1]) - 1) % peers) for i in...]
    unnamed x18 -> x10, local copies, waits for them, and re-layouts: 1.34 us -> 0.03 us
  transfers between devices with their start and end apart: 22 -> 17, of which waited for: 12 -> 10; matrix products, arithmetic and copies ran while one was open for 2% -> 0% of each run, Pallas kernels for 34% -> 33%
where the time goes in v1:
time: 82.8 us; the launch traced here: 82.5 us
  Pallas kernels  43 us (52%)
  starting transfers between devices  23.2 us (28%)
  waiting for transfers between devices  13.8 us (17%)
  between operations  1.58 us (2%)
    pallas_call x4, Pallas kernels, weight_grads(): pl.pallas_call(functools.partial(outer_kernel, tile, tuple(plan), len(ope...  17.8 us
    ppermute x10, starting transfers between devices, exchange(): return lax.ppermute(block, 'ctx', [(i, i ^ mask) for i in range(peers)])  13.2 us
    pallas_call x1, Pallas kernels, layer_pass(): pl.pallas_call(functools.partial(layer_kernel, again is not None, stream,...  10.9 us
    ppermute x10, waiting for transfers between devices, exchange(): return lax.ppermute(block, 'ctx', [(i, i ^ mask) for i in range(peers)])  9.76 us
    pallas_call x3, Pallas kernels, fetch(): pl.pallas_call(fetch_kernel, out_shape=pltpu.VMEM(weight.shape, weight.dt...  9.49 us
    ppermute x1, starting transfers between devices, scatter_sum(): lax.ppermute(sent[0], 'ctx', [(i, ((i ^ masks[-1]) - 1) % peers) for i in...  2.93 us
    ppermute x1, starting transfers between devices, first_pair(): lax.ppermute(handed, 'ctx', [(i, (i + 1) % peers) for i in range(peers)])  2.75 us
    ppermute x1, starting transfers between devices, scatter_sum(): lax.ppermute(chunks[0].astype(BF16), 'ctx', [(i, (i - 1) % peers) for i i...  2.39 us
  transfers between devices with their start and end apart: 17, of which 10 were waited for; matrix products, arithmetic and copies ran while one was open for 0% of the time, Pallas kernels for 33%

profile of v1, /device:TPU:0, one launch (start us, length us, event | category | flops | bytes accessed | tf_op | source)
XLA Modules:
  0.0 82.5 jit_solution(14786069598765856064)
XLA Ops:
  2.4 2.1 %shard_map.136 = (bf16[8,4224]{1,0:T(8,128)(2,1)S(1)}, bf16[8,4224]{1,0:T(8,128)(2,1)S(1)}) custom-call(s32[1,1,2]{2,1,0:T(1,128)} %blocks_ref.3, s32[1,1,2]{2,1,0:T(1,128)} %dest_ref.3, s32[1,1,2]{2,1,0:T(1,128)S(1)} %collective-permute-done.10.other_blocks_ref, s32[1,1,2]{2,1,0:T(1,128)S(1)} %collective-permute-done.11.other_dest_ref, ...), custom_call_target="tpu_custom_call" | custom-call | tf_op jit(solution)/shard_map/pallas_call | solution.py:197
  4.5 2.7 %collective-permute-start.12 = (bf16[8,4224]{1,0:T(8,128)(2,1)S(1)}, bf16[8,4224]{1,0:T(8,128)(2,1)S(1)}, u32[]{:S(2)}, u32[]{:S(2)}) collective-permute-start(bf16[8,4224]{1,0:T(8,128)(2,1)S(1)} %get-tuple-element.140.handed_ref), channel_id=1, source_target_pairs={{0,1},{1,2},{2,3},{3,4},{4,5},{5,6},{6,7},{7,8},{8,9},{9,10},{10,1... | collective-permute-start | bytes 202760 | tf_op jit(solution)/shard_map/ppermute | solution.py:59
  7.3 1.6 %collective-permute-start.13 = (bf16[8,4224]{1,0:T(8,128)(2,1)S(1)}, bf16[8,4224]{1,0:T(8,128)(2,1)S(1)}, u32[]{:S(2)}, u32[]{:S(2)}) collective-permute-start(bf16[8,4224]{1,0:T(8,128)(2,1)S(1)} %get-tuple-element.139.kept_ref), channel_id=1, source_target_pairs={{0,4},{1,5},{2,6},{3,7},{4,0},{5,1},{6,2},{7,3},{8,12},{9,13},{10,... | collective-permute-start | bytes 202760 | tf_op jit(solution)/shard_map/ppermute | solution.py:42
  8.8 1.4 %collective-permute-start.14 = (bf16[8,4224]{1,0:T(8,128)(2,1)S(1)}, bf16[8,4224]{1,0:T(8,128)(2,1)S(1)}, u32[]{:S(2)}, u32[]{:S(2)}) collective-permute-start(bf16[8,4224]{1,0:T(8,128)(2,1)S(1)} %get-tuple-element.140.handed_ref), channel_id=1, source_target_pairs={{0,5},{1,6},{2,7},{3,0},{4,1},{5,2},{6,3},{7,12},{8,13},{9,14},{10... | collective-permute-start | bytes 202760 | tf_op jit(solution)/shard_map/ppermute | solution.py:61
  10.2 3.2 %shard_map.137.refs_4_ = bf16[896,4096]{1,0:T(8,128)(2,1)S(1)} custom-call(bf16[896,4096]{1,0:T(8,128)(2,1)} %bitcast.31), custom_call_target="tpu_custom_call" | custom-call | bytes 7340032 | tf_op jit(solution)/shard_map/pallas_call | solution.py:406
  15.1 1.7 %collective-permute-start.15 = (bf16[2,8,4224]{2,1,0:T(8,128)(2,1)S(1)}, bf16[2,8,4224]{2,1,0:T(8,128)(2,1)S(1)}, u32[]{:S(2)}, u32[]{:S(2)}) collective-permute-start(bf16[2,8,4224]{2,1,0:T(8,128)(2,1)S(1)} %shard_map.138), channel_id=1, source_target_pairs={{0,8},{1,9},{2,10},{3,11},{4,12},{5,13},{6,14},{7,15},{8,0},{9,1},... | collective-permute-start | bytes 405512 | tf_op jit(solution)/shard_map/ppermute | solution.py:42
  16.8 3.2 %shard_map.139.refs_5_ = bf16[896,4096]{1,0:T(8,128)(2,1)S(1)} custom-call(bf16[896,4096]{1,0:T(8,128)(2,1)} %bitcast.35), custom_call_target="tpu_custom_call" | custom-call | bytes 7340032 | tf_op jit(solution)/shard_map/pallas_call | solution.py:406
  20.0 4.1 %collective-permute-done.15 = bf16[2,8,4224]{2,1,0:T(8,128)(2,1)S(1)} collective-permute-done((bf16[2,8,4224]{2,1,0:T(8,128)(2,1)S(1)}, bf16[2,8,4224]{2,1,0:T(8,128)(2,1)S(1)}, u32[]{:S(2)}, u32[]{:S(2)}) %collective-permute-start.15) | collective-permute-done | bytes 135200 | tf_op jit(solution)/shard_map/ppermute | solution.py:42
  25.3 3.2 %shard_map.140.refs_6_ = bf16[896,4096]{1,0:T(8,128)(2,1)S(1)} custom-call(bf16[896,4096]{1,0:T(8,128)(2,1)} %bitcast.39), custom_call_target="tpu_custom_call" | custom-call | bytes 7340032 | tf_op jit(solution)/shard_map/pallas_call | solution.py:406
  30.0 2.5 %collective-permute-start.19 = (bf16[8,8,2176]{2,1,0:T(8,128)(2,1)S(1)}, bf16[8,8,2176]{2,1,0:T(8,128)(2,1)S(1)}, u32[]{:S(2)}, u32[]{:S(2)}) collective-permute-start(bf16[8,8,2176]{2,1,0:T(8,128)(2,1)S(1)} %pad_maximum_fusion.2), channel_id=1, source_target_pairs={{0,2},{1,3},{2,0},{3,1},{4,6},{5,7},{6,4},{7,5},{8,10},{9,11},{10,... | collective-permute-start | bytes 835592 | tf_op jit(solution)/shard_map/ppermute | solution.py:42
  32.5 3.1 %collective-permute-done.17 = bf16[8,8,2048]{2,1,0:T(8,128)(2,1)S(1)} collective-permute-done((bf16[8,8,2048]{2,1,0:T(8,128)(2,1)S(1)}, bf16[8,8,2048]{2,1,0:T(8,128)(2,1)S(1)}, u32[]{:S(2)}, u32[]{:S(2)}) %collective-permute-start.17) | collective-permute-done | bytes 262176 | tf_op jit(solution)/shard_map/ppermute | solution.py:42
  35.7 1.4 %collective-permute-done.19 = bf16[8,8,2176]{2,1,0:T(8,128)(2,1)S(1)} collective-permute-done((bf16[8,8,2176]{2,1,0:T(8,128)(2,1)S(1)}, bf16[8,8,2176]{2,1,0:T(8,128)(2,1)S(1)}, u32[]{:S(2)}, u32[]{:S(2)}) %collective-permute-start.19) | collective-permute-done | bytes 278560 | tf_op jit(solution)/shard_map/ppermute | solution.py:42
  37.2 10.9 %shard_map.141 = (bf16[896,64]{1,0:T(8,128)(2,1)S(1)}, bf16[896,64]{1,0:T(8,128)(2,1)S(1)}, bf16[64,4096]{1,0:T(8,128)(2,1)S(1)}, f32[5,2,8,2176]{3,2,1,0:T(8,12...) custom-call(bf16[8,2,8,2048]{3,2,1,0:T(8,128)(2,1)S(1)} %bitcast.50,, ...), custom_call_target="tpu_custom_call" | custom-call | flops 2348810240 | bytes 22020096 | tf_op jit(solution)/shard_map/pallas_call | solution.py:465
  50.0 5.5 %shard_map.142 = f32[896,4096]{1,0:T(8,128)} custom-call(bf16[896,64]{1,0:T(8,128)(2,1)S(1)} %get-tuple-element.163.refs_0_, bf16[64,4096]{1,0:T(8,128)(2,1)S(1)} %get-tuple-element.164.refs_1_), custom_call_target="tpu_custom_call" | custom-call | flops 469762048 | bytes 14680064 | tf_op jit(solution)/shard_map/pallas_call | solution.py:527
  56.2 2.1 %collective-permute-start.21 = (bf16[5,8,2176]{2,1,0:T(8,128)(2,1)S(1)}, bf16[5,8,2176]{2,1,0:T(8,128)(2,1)S(1)}, u32[]{:S(2)}, u32[]{:S(2)}) collective-permute-start(bf16[5,8,2176]{2,1,0:T(8,128)(2,1)S(1)} %maximum_maximum_fusion), channel_id=1, source_target_pairs={{0,2},{1,3},{2,0},{3,1},{4,6},{5,7},{6,4},{7,5},{8,10},{9,11},{10,... | collective-permute-start | bytes 522248 | tf_op jit(solution)/shard_map/ppermute | solution.py:42
  58.3 3.7 %shard_map.143.refs_2_ = f32[896,4096]{1,0:T(8,128)} custom-call(bf16[896,64]{1,0:T(8,128)(2,1)S(1)} %get-tuple-element.173.refs_0_, bf16[64,4096]{1,0:T(8,128)(2,1)S(1)} %get-tuple-element.168.refs_1_), custom_call_target="tpu_custom_call" | custom-call | flops 268435456 | bytes 8388608 | tf_op jit(solution)/shard_map/pallas_call | solution.py:527
  62.1 1.3 %collective-permute-start.22 = (bf16[3,8,2176]{2,1,0:T(8,128)(2,1)S(1)}, bf16[3,8,2176]{2,1,0:T(8,128)(2,1)S(1)}, u32[]{:S(2)}, u32[]{:S(2)}) collective-permute-start(bf16[3,8,2176]{2,1,0:T(8,128)(2,1)S(1)} %maximum_maximum_fusion.1), channel_id=1, source_target_pairs={{0,8},{1,9},{2,10},{3,11},{4,12},{5,13},{6,14},{7,15},{8,0},{9,1},... | collective-permute-start | bytes 313352 | tf_op jit(solution)/shard_map/ppermute | solution.py:42
  63.3 4.6 %shard_map.144.refs_4_ = f32[896,4096]{1,0:T(8,128)} custom-call(bf16[896,64]{1,0:T(8,128)(2,1)S(1)} %get-tuple-element.171.refs_0_.refs_3_, bf16[64,4096]{1,0:T(8,128)(2,1)S(1)} %get-tuple-element.168.refs_1_), custom_call_target="tpu_custom_call" | custom-call | flops 369098752 | bytes 11534336 | tf_op jit(solution)/shard_map/pallas_call | solution.py:527
  68.1 2.9 %collective-permute-start.25 = (bf16[8,2176]{1,0:T(8,128)(2,1)S(1)}, bf16[8,2176]{1,0:T(8,128)(2,1)S(1)}, u32[]{:S(2)}, u32[]{:S(2)}) collective-permute-start(bf16[8,2176]{1,0:T(8,128)(2,1)S(1)} %bitcast.57), channel_id=1, source_target_pairs={{0,3},{1,4},{2,5},{3,6},{4,15},{5,0},{6,1},{7,2},{8,11},{9,12},{10... | collective-permute-start | bytes 104456 | tf_op jit(solution)/shard_map/ppermute | solution.py:119
  71.0 2.4 %collective-permute-start.24 = (bf16[8,2176]{1,0:T(8,128)(2,1)S(1)}, bf16[8,2176]{1,0:T(8,128)(2,1)S(1)}, u32[]{:S(2)}, u32[]{:S(2)}) collective-permute-start(bf16[8,2176]{1,0:T(8,128)(2,1)S(1)} %get-tuple-element.193), channel_id=1, source_target_pairs={{0,15},{1,0},{2,1},{3,2},{4,3},{5,4},{6,5},{7,6},{8,7},{9,8},{10,9... | collective-permute-start | bytes 104456 | tf_op jit(solution)/shard_map/ppermute | solution.py:116
  73.4 1.2 %collective-permute-start.23 = (bf16[2,8,2176]{2,1,0:T(8,128)(2,1)S(1)}, bf16[2,8,2176]{2,1,0:T(8,128)(2,1)S(1)}, u32[]{:S(2)}, u32[]{:S(2)}) collective-permute-start(bf16[2,8,2176]{2,1,0:T(8,128)(2,1)S(1)} %maximum_maximum_fusion.2), channel_id=1, source_target_pairs={{0,4},{1,5},{2,6},{3,7},{4,0},{5,1},{6,2},{7,3},{8,12},{9,13},{10,... | collective-permute-start | bytes 208904 | tf_op jit(solution)/shard_map/ppermute | solution.py:42
  74.6 4.0 %shard_map.145 = (f32[896,4096]{1,0:T(8,128)}, f32[896,4096]{1,0:T(8,128)}) custom-call(bf16[896,64]{1,0:T(8,128)(2,1)S(1)} %get-tuple-element.173.refs_0_, bf16[64,4096]{1,0:T(8,128)(2,1)S(1)} %get-tuple-element.168.refs_1_, f32[896,4096]{1,0:T(8,128)} %shard_map.143.refs_2_, ...), custom_call_target="tpu_custom_call", output_to_operand_aliasing={{0}: (2, {}), {1}: (4, {})} | custom-call | flops 301989888 | bytes 9437184 | tf_op jit(solution)/shard_map/pallas_call | solution.py:527
  79.4 1.3 %collective-permute-done.26.other_ref = bf16[2,8,2048]{2,1,0:T(8,128)(2,1)S(1)} collective-permute-done((bf16[2,8,2048]{2,1,0:T(8,128)(2,1)S(1)}, bf16[2,8,2048]{2,1,0:T(8,128)(2,1)S(1)}, u32[]{:S(2)}, u32[]{:S(2)}) %collective-permute-start.26) | collective-permute-done | bytes 65568 | tf_op jit(solution)/shard_map/ppermute | solution.py:735
  80.7 1.8 %shard_map.147 = bf16[128,4096]{1,0:T(8,128)(2,1)} custom-call(s32[1,1,2]{2,1,0:T(1,128)S(1)} %copy-done.1, s32[1,1,2]{2,1,0:T(1,128)S(1)} %copy-done.2, s32[1,1,2]{2,1,0:T(1,128)S(1)} %collective-permute-done.10.other_blocks_ref, s32[1,1,2]{2,1,0:T(1,128)S(1)} %collective-permute-done.11.other_dest_ref, bf16[2,8,2048]{2,1,0:T(8,128)(2,1)S(1)} %get-tuple-element.179.own_ref, ...), custom_call_target="tpu_custom_call" | custom-call | tf_op jit(solution)/shard_map/pallas_call | solution.py:681
  (56 shorter events, 9.2 us)
Async XLA Ops:
  0.6 1.5 %collective-permute-start.10 = (s32[1,1,2]{2,1,0:T(1,128)}, s32[1,1,2]{2,1,0:T(1,128)S(1)}, u32[]{:S(2)}, u32[]{:S(2)}) collective-permute-start(s32[1,1,2]{2,1,0:T(1,128)} %blocks_ref.3), channel_id=1, source_target_pairs={{0,16},{16,0},{1,17},{17,1},{2,18},{18,2},{3,19},{19,3},{4,20},{20... | collective-permute-start | bytes 32 | tf_op jit(solution)/shard_map/ppermute | solution.py:700
  1.1 1.3 %collective-permute-start.11 = (s32[1,1,2]{2,1,0:T(1,128)}, s32[1,1,2]{2,1,0:T(1,128)S(1)}, u32[]{:S(2)}, u32[]{:S(2)}) collective-permute-start(s32[1,1,2]{2,1,0:T(1,128)} %dest_ref.3), channel_id=1, source_target_pairs={{0,16},{16,0},{1,17},{17,1},{2,18},{18,2},{3,19},{19,3},{4,20},{20... | collective-permute-start | bytes 32 | tf_op jit(solution)/shard_map/ppermute | solution.py:701
  4.5 9.5 %collective-permute-start.12 = (bf16[8,4224]{1,0:T(8,128)(2,1)S(1)}, bf16[8,4224]{1,0:T(8,128)(2,1)S(1)}, u32[]{:S(2)}, u32[]{:S(2)}) collective-permute-start(bf16[8,4224]{1,0:T(8,128)(2,1)S(1)} %get-tuple-element.140.handed_ref), channel_id=1, source_target_pairs={{0,1},{1,2},{2,3},{3,4},{4,5},{5,6},{6,7},{7,8},{8,9},{9,10},{10,1... | collective-permute-start | bytes 202760 | tf_op jit(solution)/shard_map/ppermute | solution.py:59
  7.3 6.7 %collective-permute-start.13 = (bf16[8,4224]{1,0:T(8,128)(2,1)S(1)}, bf16[8,4224]{1,0:T(8,128)(2,1)S(1)}, u32[]{:S(2)}, u32[]{:S(2)}) collective-permute-start(bf16[8,4224]{1,0:T(8,128)(2,1)S(1)} %get-tuple-element.139.kept_ref), channel_id=1, source_target_pairs={{0,4},{1,5},{2,6},{3,7},{4,0},{5,1},{6,2},{7,3},{8,12},{9,13},{10,... | collective-permute-start | bytes 202760 | tf_op jit(solution)/shard_map/ppermute | solution.py:42
  8.8 6.1 %collective-permute-start.14 = (bf16[8,4224]{1,0:T(8,128)(2,1)S(1)}, bf16[8,4224]{1,0:T(8,128)(2,1)S(1)}, u32[]{:S(2)}, u32[]{:S(2)}) collective-permute-start(bf16[8,4224]{1,0:T(8,128)(2,1)S(1)} %get-tuple-element.140.handed_ref), channel_id=1, source_target_pairs={{0,5},{1,6},{2,7},{3,0},{4,1},{5,2},{6,3},{7,12},{8,13},{9,14},{10... | collective-permute-start | bytes 202760 | tf_op jit(solution)/shard_map/ppermute | solution.py:61
  15.1 9.0 %collective-permute-start.15 = (bf16[2,8,4224]{2,1,0:T(8,128)(2,1)S(1)}, bf16[2,8,4224]{2,1,0:T(8,128)(2,1)S(1)}, u32[]{:S(2)}, u32[]{:S(2)}) collective-permute-start(bf16[2,8,4224]{2,1,0:T(8,128)(2,1)S(1)} %shard_map.138), channel_id=1, source_target_pairs={{0,8},{1,9},{2,10},{3,11},{4,12},{5,13},{6,14},{7,15},{8,0},{9,1},... | collective-permute-start | bytes 405512 | tf_op jit(solution)/shard_map/ppermute | solution.py:42
  24.1 5.0 %collective-permute-start.16 = (bf16[4,8,2048]{2,1,0:T(8,128)(2,1)S(1)}, bf16[4,8,2048]{2,1,0:T(8,128)(2,1)S(1)}, u32[]{:S(2)}, u32[]{:S(2)}) collective-permute-start(bf16[4,8,2048]{2,1,0:T(8,128)(2,1)S(1)} %pad_maximum_fusion.5), channel_id=1, source_target_pairs={{0,2},{1,3},{2,0},{3,1},{4,6},{5,7},{6,4},{7,5},{8,10},{9,11},{10,... | collective-permute-start | bytes 393224 | tf_op jit(solution)/shard_map/ppermute | solution.py:42
  24.6 5.4 %collective-permute-start.18 = (bf16[4,8,2176]{2,1,0:T(8,128)(2,1)S(1)}, bf16[4,8,2176]{2,1,0:T(8,128)(2,1)S(1)}, u32[]{:S(2)}, u32[]{:S(2)}) collective-permute-start(bf16[4,8,2176]{2,1,0:T(8,128)(2,1)S(1)} %pad_maximum_fusion.4), channel_id=1, source_target_pairs={{0,1},{1,0},{2,3},{3,2},{4,5},{5,4},{6,7},{7,6},{8,9},{9,8},{10,11... | collective-permute-start | bytes 417800 | tf_op jit(solution)/shard_map/ppermute | solution.py:42
  29.2 6.4 %collective-permute-start.17 = (bf16[8,8,2048]{2,1,0:T(8,128)(2,1)S(1)}, bf16[8,8,2048]{2,1,0:T(8,128)(2,1)S(1)}, u32[]{:S(2)}, u32[]{:S(2)}) collective-permute-start(bf16[8,8,2048]{2,1,0:T(8,128)(2,1)S(1)} %pad_maximum_fusion.3), channel_id=1, source_target_pairs={{0,1},{1,0},{2,3},{3,2},{4,5},{5,4},{6,7},{7,6},{8,9},{9,8},{10,11... | collective-permute-start | bytes 786440 | tf_op jit(solution)/shard_map/ppermute | solution.py:42
  30.0 7.0 %collective-permute-start.19 = (bf16[8,8,2176]{2,1,0:T(8,128)(2,1)S(1)}, bf16[8,8,2176]{2,1,0:T(8,128)(2,1)S(1)}, u32[]{:S(2)}, u32[]{:S(2)}) collective-permute-start(bf16[8,8,2176]{2,1,0:T(8,128)(2,1)S(1)} %pad_maximum_fusion.2), channel_id=1, source_target_pairs={{0,2},{1,3},{2,0},{3,1},{4,6},{5,7},{6,4},{7,5},{8,10},{9,11},{10,... | collective-permute-start | bytes 835592 | tf_op jit(solution)/shard_map/ppermute | solution.py:42
  35.7 1.5 %copy-start.6 = (f32[1,4096]{1,0:T(1,128)S(1)}, f32[1,4096]{1,0:T(1,128)}, u32[]{:S(2)}) copy-start(f32[1,4096]{1,0:T(1,128)} %gain_ref.1) | copy-start | bytes 49156
  35.7 1.5 %copy-start.7 = (bf16[1,4096]{1,0:T(2,128)(2,1)S(1)}, bf16[1,4096]{1,0:T(2,128)(2,1)}, u32[]{:S(2)}) copy-start(bf16[1,4096]{1,0:T(2,128)(2,1)} %router_ref.1) | copy-start | bytes 24580
  49.0 7.0 %collective-permute-start.20 = (bf16[9,8,2176]{2,1,0:T(8,128)(2,1)S(1)}, bf16[9,8,2176]{2,1,0:T(8,128)(2,1)S(1)}, u32[]{:S(2)}, u32[]{:S(2)}) collective-permute-start(bf16[9,8,2176]{2,1,0:T(8,128)(2,1)S(1)} %get-tuple-element.162), channel_id=1, source_target_pairs={{0,1},{1,0},{2,3},{3,2},{4,5},{5,4},{6,7},{7,6},{8,9},{9,8},{10,11... | collective-permute-start | bytes 940040 | tf_op jit(solution)/shard_map/ppermute | solution.py:42
  56.2 5.8 %collective-permute-start.21 = (bf16[5,8,2176]{2,1,0:T(8,128)(2,1)S(1)}, bf16[5,8,2176]{2,1,0:T(8,128)(2,1)S(1)}, u32[]{:S(2)}, u32[]{:S(2)}) collective-permute-start(bf16[5,8,2176]{2,1,0:T(8,128)(2,1)S(1)} %maximum_maximum_fusion), channel_id=1, source_target_pairs={{0,2},{1,3},{2,0},{3,1},{4,6},{5,7},{6,4},{7,5},{8,10},{9,11},{10,... | collective-permute-start | bytes 522248 | tf_op jit(solution)/shard_map/ppermute | solution.py:42
  62.1 5.9 %collective-permute-start.22 = (bf16[3,8,2176]{2,1,0:T(8,128)(2,1)S(1)}, bf16[3,8,2176]{2,1,0:T(8,128)(2,1)S(1)}, u32[]{:S(2)}, u32[]{:S(2)}) collective-permute-start(bf16[3,8,2176]{2,1,0:T(8,128)(2,1)S(1)} %maximum_maximum_fusion.1), channel_id=1, source_target_pairs={{0,8},{1,9},{2,10},{3,11},{4,12},{5,13},{6,14},{7,15},{8,0},{9,1},... | collective-permute-start | bytes 313352 | tf_op jit(solution)/shard_map/ppermute | solution.py:42
  68.1 10.5 %collective-permute-start.25 = (bf16[8,2176]{1,0:T(8,128)(2,1)S(1)}, bf16[8,2176]{1,0:T(8,128)(2,1)S(1)}, u32[]{:S(2)}, u32[]{:S(2)}) collective-permute-start(bf16[8,2176]{1,0:T(8,128)(2,1)S(1)} %bitcast.57), channel_id=1, source_target_pairs={{0,3},{1,4},{2,5},{3,6},{4,15},{5,0},{6,1},{7,2},{8,11},{9,12},{10... | collective-permute-start | bytes 104456 | tf_op jit(solution)/shard_map/ppermute | solution.py:119
  71.0 7.6 %collective-permute-start.24 = (bf16[8,2176]{1,0:T(8,128)(2,1)S(1)}, bf16[8,2176]{1,0:T(8,128)(2,1)S(1)}, u32[]{:S(2)}, u32[]{:S(2)}) collective-permute-start(bf16[8,2176]{1,0:T(8,128)(2,1)S(1)} %get-tuple-element.193), channel_id=1, source_target_pairs={{0,15},{1,0},{2,1},{3,2},{4,3},{5,4},{6,5},{7,6},{8,7},{9,8},{10,9... | collective-permute-start | bytes 104456 | tf_op jit(solution)/shard_map/ppermute | solution.py:116
  73.4 5.2 %collective-permute-start.23 = (bf16[2,8,2176]{2,1,0:T(8,128)(2,1)S(1)}, bf16[2,8,2176]{2,1,0:T(8,128)(2,1)S(1)}, u32[]{:S(2)}, u32[]{:S(2)}) collective-permute-start(bf16[2,8,2176]{2,1,0:T(8,128)(2,1)S(1)} %maximum_maximum_fusion.2), channel_id=1, source_target_pairs={{0,4},{1,5},{2,6},{3,7},{4,0},{5,1},{6,2},{7,3},{8,12},{9,13},{10,... | collective-permute-start | bytes 208904 | tf_op jit(solution)/shard_map/ppermute | solution.py:42
  74.6 6.1 %copy-start = (bf16[128,4096]{1,0:T(8,128)(2,1)S(1)}, bf16[128,4096]{1,0:T(8,128)(2,1)}, u32[]{:S(2)}) copy-start(bf16[128,4096]{1,0:T(8,128)(2,1)} %grad_ref.3) | copy-start | bytes 3145732
  74.6 6.1 %copy-start.1 = (s32[1,1,2]{2,1,0:T(1,128)S(1)}, s32[1,1,2]{2,1,0:T(1,128)}, u32[]{:S(2)}) copy-start(s32[1,1,2]{2,1,0:T(1,128)} %blocks_ref.3) | copy-start | bytes 28
  74.6 6.1 %copy-start.2 = (s32[1,1,2]{2,1,0:T(1,128)S(1)}, s32[1,1,2]{2,1,0:T(1,128)}, u32[]{:S(2)}) copy-start(s32[1,1,2]{2,1,0:T(1,128)} %dest_ref.3) | copy-start | bytes 28
  79.4 1.3 %collective-permute-start.26 = (bf16[2,8,2048]{2,1,0:T(8,128)(2,1)S(1)}, bf16[2,8,2048]{2,1,0:T(8,128)(2,1)S(1)}, u32[]{:S(2)}, u32[]{:S(2)}) collective-permute-start(bf16[2,8,2048]{2,1,0:T(8,128)(2,1)S(1)} %get-tuple-element.179.own_ref), channel_id=1, source_target_pairs={{0,16},{16,0},{1,17},{17,1},{2,18},{18,2},{3,19},{19,3},{4,20},{20... | collective-permute-start | bytes 196616 | tf_op jit(solution)/shard_map/ppermute | solution.py:735
